TPU v7x, 512 devices: a whole 4x8x8 slice. The times are simulated.
512 devices in a mesh: seq: 32 (over z, x), tp: 16 (over y, core).
Axes of the slice: x: 4, y: 8, z: 8, core: 2. Of those that a mesh axis runs over, the one named last changes fastest.
Arguments:
- queries: bfloat16 [16384, 4096], P('seq', 'tp'), may hold values from -12 to 12
- keys: bfloat16 [16384, 4096], P('seq', 'tp'), may hold values from -6 to 6
- values: bfloat16 [16384, 4096], P('seq', 'tp'), may hold values from -6 to 6
- gain: bfloat16 [4096], P('tp'), may hold values from 0.25 to 1.75
- grad_out: bfloat16 [16384, 4096], P('seq', 'tp'), may hold values from -6 to 6
Outputs:
- grad_queries: bfloat16 [16384, 4096], P('seq', 'tp')
- grad_keys: bfloat16 [16384, 4096], P('seq', 'tp')
- grad_values: bfloat16 [16384, 4096], P('seq', 'tp')
All inputs are finite; a program needn't handle non-finite values.
Results may differ from a plain program's by a relative error of at most 0.0058.
Values sent between devices are 32-bit elements; how exact they have to be, the bound alone decides.
No kernel may reach another device: no remote copies, remote signals or barrier semaphores. Data moves between devices by JAX's collectives and lax.ppermute only.
A program may use at most 64 MiB of HBM per device.

v0:
```python
import jax
import jax.numpy as jnp
from jax import lax
from jax.sharding import PartitionSpec as P

HD = 128
D = 4096
BLK = 512


epsilon = 1e-06


def carried(total, later):
    place = lax.axis_index("seq")
    if later:
        add_piece = lax.all_gather(total[None], "seq", axis=0, tiled=True)
        add_index = jnp.arange(add_piece.shape[0])
        add_weight = (add_index > place).astype(jnp.float32)
        return jnp.sum(add_piece * add_weight[:, None, None, None], axis=0)
    piece = lax.all_gather(total[None], "seq", axis=0, tiled=True)
    index = jnp.arange(piece.shape[0])
    weight = (index < place).astype(jnp.float32)
    return jnp.sum(piece * weight[:, None, None, None], axis=0)


def local(queries, keys, values, gain, grad_out):
    tok_rows, width = queries.shape
    heads = width // HD
    count = tok_rows // BLK
    shape = (count, BLK, heads, HD)
    q_blocks = queries.reshape(shape)
    k_blocks = keys.reshape(shape)
    v_blocks = values.reshape(shape)
    row_index = jnp.arange(BLK)[:, None]
    col_index = jnp.arange(BLK)[None, :]
    causal = (col_index <= row_index)[None, None]

    def masked(left, right):
        scores = jnp.einsum("bthd,bshd->bhts", left, right, preferred_element_type=jnp.float32)
        return jnp.where(causal, scores, 0.0).astype(jnp.bfloat16)

    key_scores = masked(q_blocks, k_blocks)
    key_terms = jnp.einsum(
        "bshk,bshv->bhkv", k_blocks, v_blocks, preferred_element_type=jnp.float32
    )
    incoming = carried(jnp.sum(key_terms, axis=0), False)
    before = jnp.concatenate(
        [jnp.zeros_like(key_terms), jnp.cumsum(key_terms, axis=0)[:-1]], axis=0
    )
    key_state = (incoming[None] + before).astype(jnp.bfloat16)
    attn = jnp.einsum("bhts,bshd->bthd", key_scores, v_blocks, preferred_element_type=jnp.float32)
    attn = attn + jnp.einsum(
        "bthk,bhkv->bthv", q_blocks, key_state, preferred_element_type=jnp.float32
    )
    attn = attn.reshape(tok_rows, width)
    scaled = grad_out.astype(jnp.float32) * gain.astype(jnp.float32)[None, :]
    square_sum, cross = lax.psum(
        (jnp.sum(attn * attn, axis=-1), jnp.sum(scaled * attn, axis=-1)), "tp"
    )
    inv_rms = lax.rsqrt(square_sum / D + epsilon)[:, None]
    grad_attn = (scaled * inv_rms - attn * cross[:, None] * inv_rms**3 / D).astype(jnp.bfloat16)
    g_blocks = grad_attn.reshape(shape)
    grad_scores = masked(g_blocks, v_blocks)
    query_terms = jnp.einsum(
        "bthk,bthv->bhkv", q_blocks, g_blocks, preferred_element_type=jnp.float32
    )
    arriving = carried(jnp.sum(query_terms, axis=0), True)
    after_sums = jnp.cumsum(query_terms[::-1], axis=0)[::-1]
    after = jnp.concatenate([after_sums[1:], jnp.zeros_like(query_terms)], axis=0)
    grad_state = (arriving[None] + after).astype(jnp.bfloat16)
    grad_q = jnp.einsum(
        "bhts,bshk->bthk", grad_scores, k_blocks, preferred_element_type=jnp.float32
    )
    grad_q = grad_q + jnp.einsum(
        "bthv,bhkv->bthk", g_blocks, key_state, preferred_element_type=jnp.float32
    )
    key_gradient = jnp.einsum(
        "bhts,bthk->bshk", grad_scores, q_blocks, preferred_element_type=jnp.float32
    )
    key_gradient = key_gradient + jnp.einsum(
        "bshv,bhkv->bshk", v_blocks, grad_state, preferred_element_type=jnp.float32
    )
    value_gradient = jnp.einsum(
        "bhts,bthv->bshv", key_scores, g_blocks, preferred_element_type=jnp.float32
    )
    value_gradient = value_gradient + jnp.einsum(
        "bshk,bhkv->bshv", k_blocks, grad_state, preferred_element_type=jnp.float32
    )
    return (
        grad_q.reshape(tok_rows, width).astype(jnp.bfloat16),
        key_gradient.reshape(tok_rows, width).astype(jnp.bfloat16),
        value_gradient.reshape(tok_rows, width).astype(jnp.bfloat16),
    )


def solution(mesh):
    placed = (P("seq", "tp"), P("seq", "tp"), P("seq", "tp"), P("tp"), P("seq", "tp"))
    return jax.shard_map(
        local,
        mesh=mesh,
        in_specs=placed,
        out_specs=(P("seq", "tp"), P("seq", "tp"), P("seq", "tp")),
        check_vma=False,
    )
```

profile of v0, /device:TPU:6, one launch (start us, length us, event | category | flops | bytes accessed | tf_op | source)
XLA Modules:
  0.0 230.5 jit_solution(14939801349930995501)
XLA Ops:
  7.2 0.0 all-gather.5.cloned.1.call-start
  7.2 1.1 copy.109
  8.4 0.9 fusion.11
  9.2 0.0 all-gather.5.cloned.1.call-update
  9.3 0.0 all-gather.7.cloned.1.call-start
  9.3 0.7 convert_element_type.82
  10.0 1.1 copy.81
  11.1 0.1 iota_compare_fusion
  11.2 1.6 select_convert_fusion.1
  12.8 90.2 %all-gather.5.cloned.1.call-done = f32[64,128,128]{2,1,0:T(8,128)} async-done(((f32[2,128,128]{2,1,0:T(8,128)}), f32[64,128,128]{2,1,0:T(8,128)}) %all-gather.5.cloned.1.call-update) | async-done | bytes 4194320 | tf_op jit(solution)/shard_map/all_gather | solution.py:21
  103.0 2.6 %multiply_reduce_fusion.1 = bf16[2,128,128]{2,1,0:T(8,128)(2,1)S(1)} fusion(f32[32,2,128,128]{3,2,1,0:T(8,128)} %bitcast.100, f32[32]{0:T(128)S(1)} %compare_convert_fusion.1), kind=kLoop, calls=%fused_computation.1 | loop fusion | flops 2064384 | bytes 4259968 | tf_op jit(solution)/shard_map/reduce_sum | solution.py:24
  105.6 0.3 fusion.29
  105.9 0.5 fusion.6
  106.4 0.2 copy.63
  106.6 0.2 multiply_reduce_fusion.2
  106.8 23.5 %all-reduce = (f32[512]{0:T(512)S(1)}, f32[512]{0:T(512)S(1)}) all-reduce(f32[512]{0:T(512)S(1)} %get-tuple-element.16, f32[512]{0:T(512)S(1)} %multiply_reduce_fusion.2), channel_id=1, replica_groups=mesh['seq'=32,'tp'=16] {'tp'}, use_global_device_ids=true, to_apply=%region_2.3 | all-reduce | flops 1024 | bytes 8192 | tf_op jit(solution)/shard_map/psum | solution.py:58
  130.3 0.3 subtract_convert_fusion
  130.6 0.1 copy.82
  130.8 0.2 convolution_bitcast_fusion.3
  131.0 0.8 copy.71
  131.8 0.2 fusion.28
  132.0 1.5 select_convert_fusion
  133.6 1.2 fusion.3
  134.7 1.8 copy.76
  136.5 80.1 %all-gather.7.cloned.1.call-done = f32[64,128,128]{2,1,0:T(8,128)} async-done(((f32[2,128,128]{2,1,0:T(8,128)}), f32[64,128,128]{2,1,0:T(8,128)}) %all-gather.7.cloned.1.call-update) | async-done | bytes 4194320 | tf_op jit(solution)/shard_map/all_gather | solution.py:17
  216.7 2.5 %multiply_reduce_fusion = bf16[2,128,128]{2,1,0:T(8,128)(2,1)S(1)} fusion(f32[32,2,128,128]{3,2,1,0:T(8,128)} %bitcast.101, f32[32]{0:T(128)S(1)} %compare_convert_fusion), kind=kLoop, calls=%fused_computation | loop fusion | flops 2064384 | bytes 4259968 | tf_op jit(solution)/shard_map/reduce_sum | solution.py:20
  219.2 0.3 fusion.13
  219.5 0.2 fusion.8
  219.7 1.0 fusion.5
  220.8 1.8 copy.78
  222.5 0.3 fusion.4
  222.9 0.8 copy.77
  (12 shorter events, 0.1 us)
Async XLA Ops:
  7.2 1.2 copy-start
  7.2 95.9 %all-gather.5.cloned.1.call-start = ((), (), s32[]{:S(2)}) async-start(), calls=%async_computation | async-start | bytes 4325376 | tf_op jit(solution)/shard_map/all_gather | solution.py:21
  9.3 207.4 %all-gather.7.cloned.1.call-start = ((), (), s32[]{:S(2)}) async-start(), calls=%async_computation.1 | async-start | bytes 4325376 | tf_op jit(solution)/shard_map/all_gather | solution.py:17
  11.2 91.9 %copy-start.3 = (pred[512,512]{1,0:T(8,128)(4,1)}, pred[512,512]{1,0:T(8,128)(4,1)S(1)}, u32[]{:S(2)}) copy-start(pred[512,512]{1,0:T(8,128)(4,1)S(1)} %iota_compare_fusion) | copy-start | bytes 786436
  103.0 3.6 %copy-start.1 = (bf16[512,256]{1,0:T(8,128)(2,1)S(1)}, bf16[512,256]{1,0:T(8,128)(2,1)}, u32[]{:S(2)}) copy-start(bf16[512,256]{1,0:T(8,128)(2,1)} %param.9) | copy-start | bytes 786436
  132.0 87.2 %copy-start.2 = (bf16[512,256]{1,0:T(8,128)(2,1)S(1)}, bf16[512,256]{1,0:T(8,128)(2,1)}, u32[]{:S(2)}) copy-start(bf16[512,256]{1,0:T(8,128)(2,1)} %param.6) | copy-start | bytes 786436
Sparse Core Ops, SparseCore 0:
  11.8 91.2 all-gather.4
  131.9 84.7 all-gather.6
where the time goes:
time: 233 us; the launch traced here: 231 us
  waiting for transfers between devices  170 us (73%)
  blocking collectives  23.5 us (10%)
  between operations  14.2 us (6%)
  matrix products  8.19 us (4%)
  local copies, waits for them, and re-layouts  7.75 us (3%)
  other arithmetic  6.32 us (3%)
    all_gather x1, waiting for transfers between devices, carried(): piece = lax.all_gather(total[None], 'seq', axis=0, tiled=True)  90.2 us
    all_gather x1, waiting for transfers between devices, carried(): add_piece = lax.all_gather(total[None], 'seq', axis=0, tiled=True)  80.1 us
    psum x1, blocking collectives, local(): lax.psum((jnp.sum(attn * attn, axis=-1), jnp.sum(scaled * attn, axis=-1))...  23.5 us
  transfers between devices with their start and end apart: 2, of which 2 were waited for; matrix products, arithmetic and copies ran while one was open for 4% of the time, Pallas kernels for 0%

commit v1 on v0

v1 whole, which is shorter than its diff:
```python
import jax
import jax.numpy as jnp
from jax import lax
from jax.experimental import pallas as pl
from jax.experimental.pallas import tpu as pltpu
from jax.sharding import PartitionSpec as P

HD = 128
D = 4096
BLK = 512
TILE = 256
HEADS = 2
SEQ = 32
TP = 16
EPSILON = 1e-06

F32 = jnp.float32
BF16 = jnp.bfloat16
VMEM = pl.BlockSpec(memory_space=pltpu.VMEM)


def nn(a, b):
    return lax.dot_general(a, b, (((1,), (0,)), ((), ())), preferred_element_type=F32)


def nt(a, b):
    return lax.dot_general(a, b, (((1,), (1,)), ((), ())), preferred_element_type=F32)


def tn(a, b):
    return lax.dot_general(a, b, (((0,), (0,)), ((), ())), preferred_element_type=F32)


def lower():
    row = lax.broadcasted_iota(jnp.int32, (TILE, TILE), 0)
    col = lax.broadcasted_iota(jnp.int32, (TILE, TILE), 1)
    return col <= row


def upper():
    row = lax.broadcasted_iota(jnp.int32, (TILE, TILE), 0)
    col = lax.broadcasted_iota(jnp.int32, (TILE, TILE), 1)
    return col >= row


def call(kernel, outs, scratch=(), flops=0):
    return pl.pallas_call(
        kernel,
        out_shape=outs,
        scratch_shapes=list(scratch),
        compiler_params=pltpu.CompilerParams(vmem_limit_bytes=24 * 2**20),
        cost_estimate=pl.CostEstimate(flops=flops, bytes_accessed=2**20, transcendentals=0),
    )


def state_kernel(left_ref, right_ref, out_ref):
    for h in range(HEADS):
        cols = slice(h * HD, (h + 1) * HD)
        out_ref[cols, :] = tn(left_ref[:, cols], right_ref[:, cols])


def before_kernel(in_ref, out_ref):
    acc = jnp.zeros((8, 128), F32)
    for b in range(SEQ):
        out_ref[b] = acc
        acc = acc + in_ref[b]


def after_kernel(in_ref, out_ref):
    acc = jnp.zeros((8, 128), F32)
    for b in reversed(range(SEQ)):
        out_ref[b] = acc
        acc = acc + in_ref[b]


def forward_kernel(q_ref, k_ref, v_ref, gain_ref, go_ref, state_ref, attn_ref, sums_ref):
    mask = lower()
    square = []
    cross = []
    for t in range(BLK // TILE):
        rows = slice(t * TILE, (t + 1) * TILE)
        sq = jnp.zeros((TILE, HD), F32)
        cr = jnp.zeros((TILE, HD), F32)
        for h in range(HEADS):
            cols = slice(h * HD, (h + 1) * HD)
            q = q_ref[rows, cols]
            attn = nn(q, state_ref[cols, :].astype(BF16))
            for s in range(t + 1):
                srows = slice(s * TILE, (s + 1) * TILE)
                scores = nt(q, k_ref[srows, cols])
                if s == t:
                    scores = jnp.where(mask, scores, 0.0)
                attn = attn + nn(scores.astype(BF16), v_ref[srows, cols])
            attn_ref[rows, cols] = attn
            scaled = go_ref[rows, cols].astype(F32) * gain_ref[:, cols].astype(F32)
            sq = sq + attn * attn
            cr = cr + scaled * attn
        square.append(jnp.sum(sq, axis=1, keepdims=True))
        cross.append(jnp.sum(cr, axis=1, keepdims=True))
    lane = lax.broadcasted_iota(jnp.int32, (BLK, 128), 1)
    both = jnp.where(lane == 0, jnp.concatenate(square, axis=0), jnp.concatenate(cross, axis=0))
    turned = both.T
    for i in range(BLK // 128):
        part = slice(i * 128, (i + 1) * 128)
        sums_ref[:, i, :] = jnp.broadcast_to(turned[0:1, part], (TP, 128))
        sums_ref[:, i + 4, :] = jnp.broadcast_to(turned[1:2, part], (TP, 128))


def middle_kernel(q_ref, k_ref, v_ref, gain_ref, go_ref, state_ref, attn_ref, sums_ref, g_ref, gq_ref, out_ref):
    mask = lower()
    total = jnp.sum(sums_ref[...], axis=0)
    square = jnp.concatenate([total[i : i + 1] for i in range(4)], axis=1)
    cross = jnp.concatenate([total[i : i + 1] for i in range(4, 8)], axis=1)
    inv = lax.rsqrt(square / D + EPSILON)
    factor = cross * (inv * inv * inv) / D
    row = lax.broadcasted_iota(jnp.int32, (128, BLK), 0)
    turned = jnp.where(row == 0, inv, factor).T
    inv = turned[:, 0:1]
    factor = turned[:, 1:2]
    for h in range(HEADS):
        cols = slice(h * HD, (h + 1) * HD)
        scaled = go_ref[:, cols].astype(F32) * gain_ref[:, cols].astype(F32)
        g = (scaled * inv - attn_ref[:, cols] * factor).astype(BF16)
        g_ref[:, cols] = g
        out_ref[cols, :] = tn(q_ref[:, cols], g)
        state = state_ref[cols, :].astype(BF16)
        for t in range(BLK // TILE):
            rows = slice(t * TILE, (t + 1) * TILE)
            gt = g[rows]
            grad = nt(gt, state)
            for s in range(t + 1):
                srows = slice(s * TILE, (s + 1) * TILE)
                scores = nt(gt, v_ref[srows, cols])
                if s == t:
                    scores = jnp.where(mask, scores, 0.0)
                grad = grad + nn(scores.astype(BF16), k_ref[srows, cols])
            gq_ref[rows, cols] = grad.astype(BF16)


def last_kernel(q_ref, k_ref, v_ref, g_ref, state_ref, gk_ref, gv_ref):
    mask = upper()
    for h in range(HEADS):
        cols = slice(h * HD, (h + 1) * HD)
        state = state_ref[cols, :].astype(BF16)
        for s in range(BLK // TILE):
            rows = slice(s * TILE, (s + 1) * TILE)
            k = k_ref[rows, cols]
            v = v_ref[rows, cols]
            gk = nt(v, state)
            gv = nn(k, state)
            for t in range(s, BLK // TILE):
                trows = slice(t * TILE, (t + 1) * TILE)
                q = q_ref[trows, cols]
                g = g_ref[trows, cols]
                scores = nt(k, q)
                grads = nt(v, g)
                if s == t:
                    scores = jnp.where(mask, scores, 0.0)
                    grads = jnp.where(mask, grads, 0.0)
                gk = gk + nn(grads.astype(BF16), q)
                gv = gv + nn(scores.astype(BF16), g)
            gk_ref[rows, cols] = gk.astype(BF16)
            gv_ref[rows, cols] = gv.astype(BF16)


def carried(total, kernel):
    pieces = lax.all_to_all(total.reshape(SEQ, 8, 128), "seq", 0, 0, tiled=True)
    sums = call(kernel, jax.ShapeDtypeStruct((SEQ, 8, 128), F32))(pieces)
    back = lax.all_to_all(sums, "seq", 0, 0, tiled=True)
    return back.reshape(HEADS * HD, HD)


def local(queries, keys, values, gain, grad_out):
    rows, width = queries.shape
    gain = gain.reshape(1, width)
    state_shape = jax.ShapeDtypeStruct((HEADS * HD, HD), F32)
    half = jax.ShapeDtypeStruct((rows, width), BF16)
    key_terms = call(state_kernel, state_shape)(keys, values)
    key_state = carried(key_terms, before_kernel)
    attn, sums = call(
        forward_kernel,
        (jax.ShapeDtypeStruct((rows, width), F32), jax.ShapeDtypeStruct((TP, 8, 128), F32)),
    )(queries, keys, values, gain, grad_out, key_state)
    sums = lax.all_to_all(sums, "tp", 0, 0, tiled=True)
    grad_attn, grad_q, query_terms = call(middle_kernel, (half, half, state_shape))(
        queries, keys, values, gain, grad_out, key_state, attn, sums
    )
    grad_state = carried(query_terms, after_kernel)
    grad_k, grad_v = call(last_kernel, (half, half))(queries, keys, values, grad_attn, grad_state)
    return grad_q, grad_k, grad_v


def solution(mesh):
    placed = (P("seq", "tp"), P("seq", "tp"), P("seq", "tp"), P("tp"), P("seq", "tp"))
    return jax.shard_map(
        local,
        mesh=mesh,
        in_specs=placed,
        out_specs=(P("seq", "tp"), P("seq", "tp"), P("seq", "tp")),
        check_vma=False,
    )
```

time: 233 us -> 89.5 us (0.38)
  waiting for transfers between devices: 170 us -> 8.97 us
  blocking collectives: 23.5 us -> 65.2 us
  between operations: 14.2 us -> 0.71 us
  matrix products: 8.19 us -> 0 us
  Pallas kernels: 0 us -> 6.7 us
  other arithmetic: 6.32 us -> 0 us
  local copies, waits for them, and re-layouts: 7.75 us -> 1.92 us
  starting transfers between devices: 0.08 us -> 5.3 us
    all_gather x2 -> x0, waiting for transfers between devices: 170 us -> none  [the longest x1 90.2 us: carried(): piece = lax.all_gather(total[None], 'seq', axis=0, tiled=True)]
    all_to_all x0 -> x4, blocking collectives: none -> 65.2 us  [the longest x2 36.6 us: carried(): pieces = lax.all_to_all(total.reshape(SEQ, 8, 128), 'seq', 0, 0, tiled=True)]
    psum x1 -> x0, blocking collectives: 23.5 us -> none  [local(): lax.psum((jnp.sum(attn * attn, axis=-1), jnp.sum(scaled * attn, axis=-1))...]
    all_to_all x0 -> x1, waiting for transfers between devices: none -> 8.97 us  [carried(): back = lax.all_to_all(sums, 'seq', 0, 0, tiled=True)]
    dot_general x12 -> x0, matrix products: 8.19 us -> none  [the longest x2 3.14 us: masked(): jnp.einsum('bthd,bshd->bhts', left, right, preferred_element_type=jnp.flo...]
    pallas_call x0 -> x6, Pallas kernels: none -> 6.7 us  [the longest x1 2.24 us: local(): call(middle_kernel, (half, half, state_shape))]
    all_to_all x0 -> x1, starting transfers between devices: none -> 5.3 us  [carried(): back = lax.all_to_all(sums, 'seq', 0, 0, tiled=True)]
    reduce_sum x3 -> x0, other arithmetic: 5.28 us -> none  [the longest x1 2.59 us: carried(): return jnp.sum(piece * weight[:, None, None, None], axis=0)]
  transfers between devices with their start and end apart: 2 -> 1, of which waited for: 2 -> 1; matrix products, arithmetic and copies ran while one was open for 4% -> 0% of each run, Pallas kernels for 0% -> 0%
where the time goes in v1:
time: 89.5 us; the launch traced here: 88.8 us
  blocking collectives  65.2 us (73%)
  waiting for transfers between devices  8.97 us (10%)
  Pallas kernels  6.7 us (7%)
  starting transfers between devices  5.3 us (6%)
  local copies, waits for them, and re-layouts  1.92 us (2%)
    all_to_all x2, blocking collectives, carried(): pieces = lax.all_to_all(total.reshape(SEQ, 8, 128), 'seq', 0, 0, tiled=True)  36.6 us
    all_to_all x1, blocking collectives, local(): sums = lax.all_to_all(sums, 'tp', 0, 0, tiled=True)  14.9 us
    all_to_all x1, blocking collectives, carried(): back = lax.all_to_all(sums, 'seq', 0, 0, tiled=True)  13.8 us
    all_to_all x1, waiting for transfers between devices, carried(): back = lax.all_to_all(sums, 'seq', 0, 0, tiled=True)  8.97 us
    all_to_all x1, starting transfers between devices, carried(): back = lax.all_to_all(sums, 'seq', 0, 0, tiled=True)  5.3 us
    pallas_call x1, Pallas kernels, local(): call(middle_kernel, (half, half, state_shape))  2.24 us
    pallas_call x1, Pallas kernels, local(): call(last_kernel, (half, half))  2.15 us
    unnamed x14, local copies, waits for them, and re-layouts  1.92 us
  transfers between devices with their start and end apart: 1, of which 1 were waited for; matrix products, arithmetic and copies ran while one was open for 0% of the time, Pallas kernels for 0%

profile of v1, /device:TPU:6, one launch (start us, length us, event | category | flops | bytes accessed | tf_op | source)
XLA Modules:
  0.0 88.8 jit_solution(17613551803761386355)
XLA Ops:
  0.6 0.0 copy-start
  0.6 0.9 %copy-done = bf16[512,256]{1,0:T(8,128)(2,1)S(1)} copy-done((bf16[512,256]{1,0:T(8,128)(2,1)S(1)}, bf16[512,256]{1,0:T(8,128)(2,1)}, u32[]{:S(2)}) %copy-start) | copy-done | bytes 262168
  1.6 0.0 copy-start.2
  1.6 0.9 %copy-done.2 = bf16[512,256]{1,0:T(8,128)(2,1)S(1)} copy-done((bf16[512,256]{1,0:T(8,128)(2,1)S(1)}, bf16[512,256]{1,0:T(8,128)(2,1)}, u32[]{:S(2)}) %copy-start.2) | copy-done | bytes 262168
  2.5 0.0 copy-start.5
  2.5 0.3 shard_map.76
  2.8 0.0 copy-start.6
  2.8 0.0 copy-start.4
  2.8 22.3 %all_to_all.25.in_ref = f32[32,8,128]{2,1,0:T(8,128)S(1)} all-to-all(f32[32,8,128]{2,1,0:T(8,128)S(1)} %bitcast.7), channel_id=1, replica_groups=mesh['seq'=32,'tp'=16] {'seq'}, dimensions={0} | all-to-all | bytes 262144 | tf_op jit(solution)/shard_map/all_to_all | solution.py:167
  25.1 0.0 copy-start.1
  25.1 0.0 copy-start.3
  25.1 0.7 shard_map.77
  25.8 5.3 %all-to-all-start.1 = ((f32[32,8,128]{2,1,0:T(8,128)}), f32[32,8,128]{2,1,0:T(8,128)S(1)}, u32[]{:S(2)}, u32[]{:S(2)}) async-start(f32[32,8,128]{2,1,0:T(8,128)} %shard_map.77), calls=%async_computation.1 | async-start | bytes 262144 | tf_op jit(solution)/shard_map/all_to_all | solution.py:169
  31.1 0.0 copy-done.6
  31.1 9.0 %all-to-all-done.1 = f32[32,8,128]{2,1,0:T(8,128)S(1)} async-done(((f32[32,8,128]{2,1,0:T(8,128)}), f32[32,8,128]{2,1,0:T(8,128)S(1)}, u32[]{:S(2)}, u32[]{:S(2)}) %all-to-all-start.1) | async-done | bytes 131104 | tf_op jit(solution)/shard_map/all_to_all | solution.py:169
  40.1 0.0 copy-done.5
  40.1 0.0 copy-done.4
  40.1 0.0 copy-done.1
  40.1 0.0 copy-done.3
  40.1 1.3 %shard_map.78 = (f32[512,256]{1,0:T(8,128)S(1)}, f32[16,8,128]{2,1,0:T(8,128)S(1)}) custom-call(bf16[512,256]{1,0:T(8,128)(2,1)S(1)} %copy-done.4, bf16[512,256]{1,0:T(8,128)(2,1)S(1)} %copy-done.1, bf16[512,256]{1,0:T(8,128)(2,1)S(1)} %copy-done.3, bf16[1,256]{1,0:T(2,128)(2,1)S(1)} %reshape.21.gain_ref, bf16[512,256]{1,0:T(8,128)(2,1)S(1)} %copy-done.5, ...), custom_call_target="tpu_custom_call" | custom-call | bytes 1048576 | tf_op jit(solution)/shard_map/pallas_call | solution.py:180
  41.4 14.9 %all_to_all.26.sums_ref = f32[16,8,128]{2,1,0:T(8,128)S(1)} all-to-all(f32[16,8,128]{2,1,0:T(8,128)S(1)} %get-tuple-element.11), channel_id=1, replica_groups=mesh['seq'=32,'tp'=16] {'tp'}, dimensions={0} | all-to-all | bytes 131072 | tf_op jit(solution)/shard_map/all_to_all | solution.py:184
  56.3 2.2 %shard_map.79 = (bf16[512,256]{1,0:T(8,128)(2,1)S(1)}, bf16[512,256]{1,0:T(8,128)(2,1)}, f32[256,128]{1,0:T(8,128)S(1)}) custom-call(bf16[512,256]{1,0:T(8,128)(2,1)S(1)} %copy-done.4, bf16[512,256]{1,0:T(8,128)(2,1)S(1)} %copy-done.1, bf16[512,256]{1,0:T(8,128)(2,1)S(1)} %copy-done.3, bf16[1,256]{1,0:T(2,128)(2,1)S(1)} %reshape.21.gain_ref, ...), custom_call_target="tpu_custom_call" | custom-call | bytes 1048576 | tf_op jit(solution)/shard_map/pallas_call | solution.py:185
  58.6 14.3 %all_to_all.27.in_ref = f32[32,8,128]{2,1,0:T(8,128)S(1)} all-to-all(f32[32,8,128]{2,1,0:T(8,128)S(1)} %bitcast.8), channel_id=1, replica_groups=mesh['seq'=32,'tp'=16] {'seq'}, dimensions={0} | all-to-all | bytes 262144 | tf_op jit(solution)/shard_map/all_to_all | solution.py:167
  72.9 13.8 %all_to_all.28 = f32[32,8,128]{2,1,0:T(8,128)S(1)} all-to-all(f32[32,8,128]{2,1,0:T(8,128)S(1)} %shard_map.80), channel_id=1, replica_groups=mesh['seq'=32,'tp'=16] {'seq'}, dimensions={0} | all-to-all | bytes 262144 | tf_op jit(solution)/shard_map/all_to_all | solution.py:169
  86.7 2.2 %shard_map.81 = (bf16[512,256]{1,0:T(8,128)(2,1)}, bf16[512,256]{1,0:T(8,128)(2,1)}) custom-call(bf16[512,256]{1,0:T(8,128)(2,1)S(1)} %copy-done.4, bf16[512,256]{1,0:T(8,128)(2,1)S(1)} %copy-done.1, bf16[512,256]{1,0:T(8,128)(2,1)S(1)} %copy-done.3, bf16[512,256]{1,0:T(8,128)(2,1)S(1)} %get-tuple-element.13.g_ref, f32[256,128]{1,0:T(8,128)S(1)} %bitcast.6), custom_call_target="tpu_custom_call" | custom-call | bytes 1048576 | tf_op jit(solution)/shard_map/pallas_call | solution.py:189
  (2 shorter events, 0.0 us)
Async XLA Ops:
  0.6 1.0 %copy-start = (bf16[512,256]{1,0:T(8,128)(2,1)S(1)}, bf16[512,256]{1,0:T(8,128)(2,1)}, u32[]{:S(2)}) copy-start(bf16[512,256]{1,0:T(8,128)(2,1)} %k_ref.5) | copy-start | bytes 786436
  1.6 0.9 %copy-start.2 = (bf16[512,256]{1,0:T(8,128)(2,1)S(1)}, bf16[512,256]{1,0:T(8,128)(2,1)}, u32[]{:S(2)}) copy-start(bf16[512,256]{1,0:T(8,128)(2,1)} %v_ref.5) | copy-start | bytes 786436
  2.5 37.6 %copy-start.5 = (bf16[512,256]{1,0:T(8,128)(2,1)S(1)}, bf16[512,256]{1,0:T(8,128)(2,1)}, u32[]{:S(2)}) copy-start(bf16[512,256]{1,0:T(8,128)(2,1)} %go_ref.3) | copy-start | bytes 786436
  2.8 28.3 %copy-start.6 = (bf16[256]{0:T(256)(128)(2,1)S(1)}, bf16[256]{0:T(256)(128)(2,1)}, u32[]{:S(2)}) copy-start(bf16[256]{0:T(256)(128)(2,1)} %param.8) | copy-start | bytes 1540
  2.8 37.3 %copy-start.4 = (bf16[512,256]{1,0:T(8,128)(2,1)S(1)}, bf16[512,256]{1,0:T(8,128)(2,1)}, u32[]{:S(2)}) copy-start(bf16[512,256]{1,0:T(8,128)(2,1)} %q_ref.5) | copy-start | bytes 786436
  25.1 15.0 %copy-start.1 = (bf16[512,256]{1,0:T(8,128)(2,1)S(1)}, bf16[512,256]{1,0:T(8,128)(2,1)}, u32[]{:S(2)}) copy-start(bf16[512,256]{1,0:T(8,128)(2,1)} %k_ref.5) | copy-start | bytes 786436
  25.1 15.0 %copy-start.3 = (bf16[512,256]{1,0:T(8,128)(2,1)S(1)}, bf16[512,256]{1,0:T(8,128)(2,1)}, u32[]{:S(2)}) copy-start(bf16[512,256]{1,0:T(8,128)(2,1)} %v_ref.5) | copy-start | bytes 786436
  25.8 14.3 %all-to-all-start.1 = ((f32[32,8,128]{2,1,0:T(8,128)}), f32[32,8,128]{2,1,0:T(8,128)S(1)}, u32[]{:S(2)}, u32[]{:S(2)}) async-start(f32[32,8,128]{2,1,0:T(8,128)} %shard_map.77), calls=%async_computation.1 | async-start | bytes 262144 | tf_op jit(solution)/shard_map/all_to_all | solution.py:169

commit v2 on v1

v2 whole, which is shorter than its diff:
```python
import jax
import jax.numpy as jnp
from jax import lax
from jax.experimental import pallas as pl
from jax.experimental.pallas import tpu as pltpu
from jax.sharding import PartitionSpec as P

HD = 128
D = 4096
BLK = 512
TILE = 256
HEADS = 2
WIDTH = HEADS * HD
SEQ = 32
TP = 16
CHUNKS = 4
EPSILON = 1e-06

F32 = jnp.float32
BF16 = jnp.bfloat16


def nn(a, b):
    return lax.dot_general(a, b, (((1,), (0,)), ((), ())), preferred_element_type=F32)


def nt(a, b):
    return lax.dot_general(a, b, (((1,), (1,)), ((), ())), preferred_element_type=F32)


def tn(a, b):
    return lax.dot_general(a, b, (((0,), (0,)), ((), ())), preferred_element_type=F32)


def head(h):
    return slice(h * HD, (h + 1) * HD)


def tile(t):
    return slice(t * TILE, (t + 1) * TILE)


def masks():
    row = lax.broadcasted_iota(jnp.int32, (TILE, TILE), 0)
    col = lax.broadcasted_iota(jnp.int32, (TILE, TILE), 1)
    return col <= row, col >= row


def call(kernel, outs, flops, moved, limit=16, **spec):
    return pl.pallas_call(
        kernel,
        out_shape=outs,
        compiler_params=pltpu.CompilerParams(vmem_limit_bytes=limit * 2**20),
        cost_estimate=pl.CostEstimate(flops=flops, bytes_accessed=moved, transcendentals=0),
        **spec,
    )


def state_kernel(k_hbm, v_hbm, out_ref, k_ref, v_ref, sems):
    copies = []
    for c in range(CHUNKS):
        rows = pl.ds(c * (BLK // CHUNKS), BLK // CHUNKS)
        pair = (
            pltpu.make_async_copy(k_hbm.at[rows], k_ref.at[rows], sems.at[0, c]),
            pltpu.make_async_copy(v_hbm.at[rows], v_ref.at[rows], sems.at[1, c]),
        )
        for copy in pair:
            copy.start()
        copies.append(pair)
    total = [None] * HEADS
    for c in range(CHUNKS):
        for copy in copies[c]:
            copy.wait()
        rows = slice(c * (BLK // CHUNKS), (c + 1) * (BLK // CHUNKS))
        for h in range(HEADS):
            term = tn(v_ref[rows, head(h)], k_ref[rows, head(h)])
            total[h] = term if c == 0 else total[h] + term
    for h in range(HEADS):
        out_ref[head(h), :] = total[h]


def before_kernel(in_ref, out_ref):
    acc = jnp.zeros((8, 128), F32)
    for b in range(SEQ):
        out_ref[b] = acc
        acc = acc + in_ref[b]


def after_kernel(in_ref, out_ref):
    acc = jnp.zeros((8, 128), F32)
    for b in reversed(range(SEQ)):
        out_ref[b] = acc
        acc = acc + in_ref[b]


def local_kernel(q_ref, k_ref, v_ref, gain_ref, go_ref, inner_ref, scaled_ref):
    lower, _ = masks()
    scaled_ref[...] = (go_ref[...].astype(F32) * gain_ref[...].astype(F32)).T
    for h in range(HEADS):
        for t in range(BLK // TILE):
            attn = None
            for s in range(t + 1):
                scores = nt(q_ref[tile(t), head(h)], k_ref[tile(s), head(h)])
                if s == t:
                    scores = jnp.where(lower, scores, 0.0)
                term = nn(scores.astype(BF16), v_ref[tile(s), head(h)])
                attn = term if attn is None else attn + term
            inner_ref[head(h), tile(t)] = attn.T


def attn_kernel(q_ref, inner_ref, scaled_ref, state_ref, attn_ref, sums_ref):
    square = jnp.zeros((8, BLK), F32)
    cross = jnp.zeros((8, BLK), F32)
    for h in range(HEADS):
        attn = inner_ref[head(h), :] + nt(state_ref[head(h), :].astype(BF16), q_ref[:, head(h)])
        attn_ref[head(h), :] = attn
        square = square + jnp.sum((attn * attn).reshape(HD // 8, 8, BLK), axis=0)
        cross = cross + jnp.sum((scaled_ref[head(h), :] * attn).reshape(HD // 8, 8, BLK), axis=0)
    square = jnp.sum(square, axis=0, keepdims=True)
    cross = jnp.sum(cross, axis=0, keepdims=True)
    rows = [x[:, i * 128 : (i + 1) * 128] for x in (square, cross) for i in range(BLK // 128)]
    sums_ref[...] = jnp.broadcast_to(jnp.concatenate(rows, axis=0)[None], (TP, 8, 128))


def grad_kernel(q_ref, scaled_ref, attn_ref, sums_ref, g_ref, out_ref):
    total = jnp.sum(sums_ref[...], axis=0)
    inv = lax.rsqrt(total[0:4] / D + EPSILON)
    factor = total[4:8] * (inv * inv * inv) / D
    inv = jnp.concatenate([inv[i : i + 1] for i in range(BLK // 128)], axis=1)
    factor = jnp.concatenate([factor[i : i + 1] for i in range(BLK // 128)], axis=1)
    for h in range(HEADS):
        g = (scaled_ref[head(h), :] * inv - attn_ref[head(h), :] * factor).astype(BF16)
        g_ref[head(h), :] = g
        out_ref[head(h), :] = nn(g, q_ref[:, head(h)])


def inner_kernel(q_ref, k_ref, v_ref, g_ref, state_ref, gq_ref, gk_ref, gv_ref):
    lower, upper = masks()
    for h in range(HEADS):
        g = g_ref[head(h), :].T
        state = state_ref[head(h), :].astype(BF16)
        for t in range(BLK // TILE):
            grad = nn(g[tile(t)], state)
            for s in range(t + 1):
                scores = nt(g[tile(t)], v_ref[tile(s), head(h)])
                if s == t:
                    scores = jnp.where(lower, scores, 0.0)
                grad = grad + nn(scores.astype(BF16), k_ref[tile(s), head(h)])
            gq_ref[tile(t), head(h)] = grad.astype(BF16)
        for s in range(BLK // TILE):
            gk = gv = None
            for t in range(s, BLK // TILE):
                q = q_ref[tile(t), head(h)]
                scores = nt(k_ref[tile(s), head(h)], q)
                grads = nn(v_ref[tile(s), head(h)], g_ref[head(h), tile(t)])
                if s == t:
                    scores = jnp.where(upper, scores, 0.0)
                    grads = jnp.where(upper, grads, 0.0)
                gk_term = nn(grads.astype(BF16), q)
                gv_term = nn(scores.astype(BF16), g[tile(t)])
                gk = gk_term if gk is None else gk + gk_term
                gv = gv_term if gv is None else gv + gv_term
            gk_ref[tile(s), head(h)] = gk
            gv_ref[tile(s), head(h)] = gv


def last_kernel(k_ref, v_ref, gk_in_ref, gv_in_ref, state_ref, gk_ref, gv_ref):
    for h in range(HEADS):
        state = state_ref[head(h), :].astype(BF16)
        gk_ref[:, head(h)] = (gk_in_ref[:, head(h)] + nn(v_ref[:, head(h)], state)).astype(BF16)
        gv_ref[:, head(h)] = (gv_in_ref[:, head(h)] + nt(k_ref[:, head(h)], state)).astype(BF16)


def carried(total, kernel):
    pieces = lax.all_to_all(total.reshape(SEQ, 8, 128), "seq", 0, 0, tiled=True)
    sums = call(kernel, jax.ShapeDtypeStruct((SEQ, 8, 128), F32), 2**15, 2**18)(pieces)
    back = lax.all_to_all(sums, "seq", 0, 0, tiled=True)
    return back.reshape(WIDTH, HD)


def local(queries, keys, values, gain, grad_out):
    gain = gain.reshape(1, WIDTH)
    state_shape = jax.ShapeDtypeStruct((WIDTH, HD), F32)
    half = jax.ShapeDtypeStruct((BLK, WIDTH), BF16)
    full = jax.ShapeDtypeStruct((BLK, WIDTH), F32)
    half_turned = jax.ShapeDtypeStruct((WIDTH, BLK), BF16)
    full_turned = jax.ShapeDtypeStruct((WIDTH, BLK), F32)
    small = 2 * HEADS * BLK * HD * HD
    square = 2 * HEADS * BLK * BLK * HD
    key_terms = call(
        state_kernel,
        state_shape,
        small,
        2**19,
        limit=60,
        in_specs=[pl.BlockSpec(memory_space=pltpu.HBM)] * 2,
        scratch_shapes=[
            pltpu.VMEM((BLK, WIDTH), BF16),
            pltpu.VMEM((BLK, WIDTH), BF16),
            pltpu.SemaphoreType.DMA((2, CHUNKS)),
        ],
    )(keys, values)
    key_state = carried(key_terms, before_kernel)
    inner, scaled = call(local_kernel, (full_turned, full_turned), 2 * square, 2**21)(
        queries, keys, values, gain, grad_out
    )
    attn, sums = call(
        attn_kernel, (full_turned, jax.ShapeDtypeStruct((TP, 8, 128), F32)), small, 2**21
    )(queries, inner, scaled, key_state)
    sums = lax.all_to_all(sums, "tp", 0, 0, tiled=True)
    grad_attn, query_terms = call(grad_kernel, (half_turned, state_shape), small, 2**21)(
        queries, scaled, attn, sums
    )
    grad_state = carried(query_terms, after_kernel)
    grad_q, inner_k, inner_v = call(inner_kernel, (half, full, full), 6 * square, 2**22)(
        queries, keys, values, grad_attn, key_state
    )
    grad_k, grad_v = call(last_kernel, (half, half), 2 * small, 2**21)(
        keys, values, inner_k, inner_v, grad_state
    )
    return grad_q, grad_k, grad_v


def solution(mesh):
    placed = (P("seq", "tp"), P("seq", "tp"), P("seq", "tp"), P("tp"), P("seq", "tp"))
    return jax.shard_map(
        local,
        mesh=mesh,
        in_specs=placed,
        out_specs=(P("seq", "tp"), P("seq", "tp"), P("seq", "tp")),
        check_vma=False,
    )
```

time: 89.5 us -> 86.9 us (0.971)
  blocking collectives: 65.2 us -> 51.7 us
  waiting for transfers between devices: 8.97 us -> 14.6 us
  starting transfers between devices: 5.3 us -> 10.8 us
  local copies, waits for them, and re-layouts: 1.92 us -> 0.03 us
  Pallas kernels: 6.7 us -> 8.38 us
    all_to_all x1 -> x0, blocking collectives: 13.8 us -> none  [carried(): back = lax.all_to_all(sums, 'seq', 0, 0, tiled=True)]
    all_to_all x1 -> x2, waiting for transfers between devices: 8.97 us -> 14.6 us  [carried(): back = lax.all_to_all(sums, 'seq', 0, 0, tiled=True)]
    all_to_all x1 -> x2, starting transfers between devices: 5.3 us -> 10.8 us  [carried(): back = lax.all_to_all(sums, 'seq', 0, 0, tiled=True)]
    unnamed x14 -> x10, local copies, waits for them, and re-layouts: 1.92 us -> 0.02 us
    pallas_call x6 -> x8, Pallas kernels: 6.7 us -> 8.38 us  [the longest x1 2.39 us: local(): call(inner_kernel, (half, full, full), 6 * square, 2 ** 22)]
  transfers between devices with their start and end apart: 1 -> 2, of which waited for: 1 -> 2; matrix products, arithmetic and copies ran while one was open for 0% -> 0% of each run, Pallas kernels for 0% -> 4%
where the time goes in v2:
time: 86.9 us; the launch traced here: 86.2 us
  blocking collectives  51.7 us (59%)
  waiting for transfers between devices  14.6 us (17%)
  starting transfers between devices  10.8 us (12%)
  Pallas kernels  8.38 us (10%)
    all_to_all x2, blocking collectives, carried(): pieces = lax.all_to_all(total.reshape(SEQ, 8, 128), 'seq', 0, 0, tiled=True)  36.8 us
    all_to_all x1, blocking collectives, local(): sums = lax.all_to_all(sums, 'tp', 0, 0, tiled=True)  14.9 us
    all_to_all x2, waiting for transfers between devices, carried(): back = lax.all_to_all(sums, 'seq', 0, 0, tiled=True)  14.6 us
    all_to_all x2, starting transfers between devices, carried(): back = lax.all_to_all(sums, 'seq', 0, 0, tiled=True)  10.8 us
    pallas_call x1, Pallas kernels, local(): call(inner_kernel, (half, full, full), 6 * square, 2 ** 22)  2.39 us
    pallas_call x1, Pallas kernels, local(): call(state_kernel, state_shape, small, 2 ** 19, limit=60, in_specs=[pl.Bl...  2.09 us
  transfers between devices with their start and end apart: 2, of which 2 were waited for; matrix products, arithmetic and copies ran while one was open for 0% of the time, Pallas kernels for 4%

profile of v2, /device:TPU:6, one launch (start us, length us, event | category | flops | bytes accessed | tf_op | source)
XLA Modules:
  0.0 86.2 jit_solution(7226560626000512759)
XLA Ops:
  0.6 0.0 copy-start.3
  0.6 2.1 %shard_map.77 = f32[256,128]{1,0:T(8,128)} custom-call(bf16[512,256]{1,0:T(8,128)(2,1)} %k_ref.5, bf16[512,256]{1,0:T(8,128)(2,1)} %v_ref.5), custom_call_target="tpu_custom_call" | custom-call | flops 33554432 | bytes 524288 | tf_op jit(solution)/shard_map/pallas_call | solution.py:190
  2.7 0.0 copy-start.4
  2.7 0.0 copy-start.2
  2.8 22.5 %all_to_all.25.in_ref = f32[32,8,128]{2,1,0:T(8,128)S(1)} all-to-all(f32[32,8,128]{2,1,0:T(8,128)} %bitcast.8), channel_id=1, replica_groups=mesh['seq'=32,'tp'=16] {'seq'}, dimensions={0} | all-to-all | bytes 262144 | tf_op jit(solution)/shard_map/all_to_all | solution.py:175
  25.2 0.0 copy-start
  25.2 0.0 copy-start.1
  25.2 0.7 shard_map.78
  25.9 5.3 %all-to-all-start.1 = ((f32[32,8,128]{2,1,0:T(8,128)}), f32[32,8,128]{2,1,0:T(8,128)S(1)}, u32[]{:S(2)}, u32[]{:S(2)}) async-start(f32[32,8,128]{2,1,0:T(8,128)} %shard_map.78), calls=%async_computation.1 | async-start | bytes 262144 | tf_op jit(solution)/shard_map/all_to_all | solution.py:177
  31.2 0.0 copy-done.4
  31.2 0.0 copy-done.3
  31.3 0.0 copy-done.2
  31.3 0.0 copy-done
  31.3 0.0 copy-done.1
  31.3 0.9 %shard_map.76 = (f32[256,512]{1,0:T(8,128)S(1)}, f32[256,512]{1,0:T(8,128)S(1)}) custom-call(bf16[512,256]{1,0:T(8,128)(2,1)S(1)} %copy-done.2, bf16[512,256]{1,0:T(8,128)(2,1)S(1)} %copy-done, bf16[512,256]{1,0:T(8,128)(2,1)S(1)} %copy-done.1, bf16[1,256]{1,0:T(2,128)(2,1)S(1)} %reshape.21.gain_ref, bf16[512,256]{1,0:T(8,128)(2,1)S(1)} %copy-done.3), custom_call_target="tpu_custom_call" | custom-call | flops 268435456 | bytes 2097152 | tf_op jit(solution)/shard_map/pallas_call | solution.py:204
  32.2 8.0 %all-to-all-done.1 = f32[32,8,128]{2,1,0:T(8,128)S(1)} async-done(((f32[32,8,128]{2,1,0:T(8,128)}), f32[32,8,128]{2,1,0:T(8,128)S(1)}, u32[]{:S(2)}, u32[]{:S(2)}) %all-to-all-start.1) | async-done | bytes 131104 | tf_op jit(solution)/shard_map/all_to_all | solution.py:177
  40.2 0.3 shard_map.79
  40.5 14.9 %all_to_all.26.sums_ref = f32[16,8,128]{2,1,0:T(8,128)S(1)} all-to-all(f32[16,8,128]{2,1,0:T(8,128)S(1)} %get-tuple-element.17), channel_id=1, replica_groups=mesh['seq'=32,'tp'=16] {'tp'}, dimensions={0} | all-to-all | bytes 131072 | tf_op jit(solution)/shard_map/all_to_all | solution.py:210
  55.4 0.2 shard_map.80
  55.6 14.3 %all_to_all.27.in_ref = f32[32,8,128]{2,1,0:T(8,128)S(1)} all-to-all(f32[32,8,128]{2,1,0:T(8,128)S(1)} %bitcast.7), channel_id=1, replica_groups=mesh['seq'=32,'tp'=16] {'seq'}, dimensions={0} | all-to-all | bytes 262144 | tf_op jit(solution)/shard_map/all_to_all | solution.py:175
  69.9 0.7 shard_map.82
  70.6 5.5 %all-to-all-start.4 = ((f32[32,8,128]{2,1,0:T(8,128)}), f32[32,8,128]{2,1,0:T(8,128)S(1)}, u32[]{:S(2)}, u32[]{:S(2)}) async-start(f32[32,8,128]{2,1,0:T(8,128)} %shard_map.82), calls=%async_computation.4 | async-start | bytes 262144 | tf_op jit(solution)/shard_map/all_to_all | solution.py:177
  76.1 2.4 %shard_map.81 = (bf16[512,256]{1,0:T(8,128)(2,1)}, f32[512,256]{1,0:T(8,128)S(1)}, f32[512,256]{1,0:T(8,128)S(1)}) custom-call(bf16[512,256]{1,0:T(8,128)(2,1)S(1)} %copy-done.2, bf16[512,256]{1,0:T(8,128)(2,1)S(1)} %copy-done, bf16[512,256]{1,0:T(8,128)(2,1)S(1)} %copy-done.1, bf16[256,512]{1,0:T(8,128)(2,1)S(1)} %get-tuple-element.18.g_ref, ...), custom_call_target="tpu_custom_call" | custom-call | flops 805306368 | bytes 4194304 | tf_op jit(solution)/shard_map/pallas_call | solution.py:215
  78.5 6.6 %all-to-all-done.4 = f32[32,8,128]{2,1,0:T(8,128)S(1)} async-done(((f32[32,8,128]{2,1,0:T(8,128)}), f32[32,8,128]{2,1,0:T(8,128)S(1)}, u32[]{:S(2)}, u32[]{:S(2)}) %all-to-all-start.4) | async-done | bytes 131104 | tf_op jit(solution)/shard_map/all_to_all | solution.py:177
  85.1 1.1 %shard_map.83 = (bf16[512,256]{1,0:T(8,128)(2,1)}, bf16[512,256]{1,0:T(8,128)(2,1)}) custom-call(bf16[512,256]{1,0:T(8,128)(2,1)S(1)} %copy-done, bf16[512,256]{1,0:T(8,128)(2,1)S(1)} %copy-done.1, f32[512,256]{1,0:T(8,128)S(1)} %get-tuple-element.20.gk_in_ref, f32[512,256]{1,0:T(8,128)S(1)} %get-tuple-element.21.gv_in_ref, f32[256,128]{1,0:T(8,128)S(1)} %bitcast.6), custom_call_target="tpu_custom_call" | custom-call | flops 67108864 | bytes 2097152 | tf_op jit(solution)/shard_map/pallas_call | solution.py:218
  (1 shorter events, 0.0 us)
Async XLA Ops:
  0.6 30.6 %copy-start.3 = (bf16[512,256]{1,0:T(8,128)(2,1)S(1)}, bf16[512,256]{1,0:T(8,128)(2,1)}, u32[]{:S(2)}) copy-start(bf16[512,256]{1,0:T(8,128)(2,1)} %go_ref.1) | copy-start | bytes 786436
  2.7 28.5 %copy-start.4 = (bf16[256]{0:T(256)(128)(2,1)S(1)}, bf16[256]{0:T(256)(128)(2,1)}, u32[]{:S(2)}) copy-start(bf16[256]{0:T(256)(128)(2,1)} %param.8) | copy-start | bytes 1540
  2.7 28.5 %copy-start.2 = (bf16[512,256]{1,0:T(8,128)(2,1)S(1)}, bf16[512,256]{1,0:T(8,128)(2,1)}, u32[]{:S(2)}) copy-start(bf16[512,256]{1,0:T(8,128)(2,1)} %q_ref.7) | copy-start | bytes 786436
  25.2 6.0 %copy-start = (bf16[512,256]{1,0:T(8,128)(2,1)S(1)}, bf16[512,256]{1,0:T(8,128)(2,1)}, u32[]{:S(2)}) copy-start(bf16[512,256]{1,0:T(8,128)(2,1)} %k_ref.5) | copy-start | bytes 786436
  25.2 6.0 %copy-start.1 = (bf16[512,256]{1,0:T(8,128)(2,1)S(1)}, bf16[512,256]{1,0:T(8,128)(2,1)}, u32[]{:S(2)}) copy-start(bf16[512,256]{1,0:T(8,128)(2,1)} %v_ref.5) | copy-start | bytes 786436
  25.9 14.3 %all-to-all-start.1 = ((f32[32,8,128]{2,1,0:T(8,128)}), f32[32,8,128]{2,1,0:T(8,128)S(1)}, u32[]{:S(2)}, u32[]{:S(2)}) async-start(f32[32,8,128]{2,1,0:T(8,128)} %shard_map.78), calls=%async_computation.1 | async-start | bytes 262144 | tf_op jit(solution)/shard_map/all_to_all | solution.py:177
  70.6 14.5 %all-to-all-start.4 = ((f32[32,8,128]{2,1,0:T(8,128)}), f32[32,8,128]{2,1,0:T(8,128)S(1)}, u32[]{:S(2)}, u32[]{:S(2)}) async-start(f32[32,8,128]{2,1,0:T(8,128)} %shard_map.82), calls=%async_computation.4 | async-start | bytes 262144 | tf_op jit(solution)/shard_map/all_to_all | solution.py:177

commit v3 on v2

--- a/solution.py
+++ b/solution.py
@@ -13,7 +13,6 @@
 WIDTH = HEADS * HD
 SEQ = 32
 TP = 16
-CHUNKS = 4
 EPSILON = 1e-06
 
 F32 = jnp.float32
@@ -57,26 +56,16 @@
 
 
 def state_kernel(k_hbm, v_hbm, out_ref, k_ref, v_ref, sems):
-    copies = []
-    for c in range(CHUNKS):
-        rows = pl.ds(c * (BLK // CHUNKS), BLK // CHUNKS)
-        pair = (
-            pltpu.make_async_copy(k_hbm.at[rows], k_ref.at[rows], sems.at[0, c]),
-            pltpu.make_async_copy(v_hbm.at[rows], v_ref.at[rows], sems.at[1, c]),
-        )
-        for copy in pair:
-            copy.start()
-        copies.append(pair)
-    total = [None] * HEADS
-    for c in range(CHUNKS):
-        for copy in copies[c]:
-            copy.wait()
-        rows = slice(c * (BLK // CHUNKS), (c + 1) * (BLK // CHUNKS))
-        for h in range(HEADS):
-            term = tn(v_ref[rows, head(h)], k_ref[rows, head(h)])
-            total[h] = term if c == 0 else total[h] + term
-    for h in range(HEADS):
-        out_ref[head(h), :] = total[h]
+    copies = (
+        pltpu.make_async_copy(k_hbm, k_ref, sems.at[0]),
+        pltpu.make_async_copy(v_hbm, v_ref, sems.at[1]),
+    )
+    for copy in copies:
+        copy.start()
+    for copy in copies:
+        copy.wait()
+    for h in range(HEADS):
+        out_ref[head(h), :] = tn(v_ref[:, head(h)], k_ref[:, head(h)])
 
 
 def before_kernel(in_ref, out_ref):
@@ -164,23 +153,32 @@
             gv_ref[tile(s), head(h)] = gv
 
 
-def last_kernel(k_ref, v_ref, gk_in_ref, gv_in_ref, state_ref, gk_ref, gv_ref):
-    for h in range(HEADS):
-        state = state_ref[head(h), :].astype(BF16)
-        gk_ref[:, head(h)] = (gk_in_ref[:, head(h)] + nn(v_ref[:, head(h)], state)).astype(BF16)
-        gv_ref[:, head(h)] = (gv_in_ref[:, head(h)] + nt(k_ref[:, head(h)], state)).astype(BF16)
+def last_kernel(k_ref, v_ref, gk_in_ref, gv_in_ref, state_ref, gk_hbm, gv_hbm, gk_ref, gv_ref, sems):
+    state = [state_ref[head(h), :].astype(BF16) for h in range(HEADS)]
+    copies = []
+    for t in range(BLK // TILE):
+        for h in range(HEADS):
+            gk = gk_in_ref[tile(t), head(h)] + nn(v_ref[tile(t), head(h)], state[h])
+            gk_ref[tile(t), head(h)] = gk.astype(BF16)
+            gv = gv_in_ref[tile(t), head(h)] + nt(k_ref[tile(t), head(h)], state[h])
+            gv_ref[tile(t), head(h)] = gv.astype(BF16)
+        for i, (mine, out) in enumerate(((gk_ref, gk_hbm), (gv_ref, gv_hbm))):
+            copies.append(pltpu.make_async_copy(mine.at[tile(t)], out.at[tile(t)], sems.at[i, t]))
+            copies[-1].start()
+    for copy in copies:
+        copy.wait()
 
 
 def carried(total, kernel):
     pieces = lax.all_to_all(total.reshape(SEQ, 8, 128), "seq", 0, 0, tiled=True)
-    sums = call(kernel, jax.ShapeDtypeStruct((SEQ, 8, 128), F32), 2**15, 2**18)(pieces)
+    sums = call(kernel, pltpu.VMEM((SEQ, 8, 128), F32), 2**15, 2**18)(pieces)
     back = lax.all_to_all(sums, "seq", 0, 0, tiled=True)
     return back.reshape(WIDTH, HD)
 
 
 def local(queries, keys, values, gain, grad_out):
     gain = gain.reshape(1, WIDTH)
-    state_shape = jax.ShapeDtypeStruct((WIDTH, HD), F32)
+    state_shape = pltpu.VMEM((WIDTH, HD), F32)
     half = jax.ShapeDtypeStruct((BLK, WIDTH), BF16)
     full = jax.ShapeDtypeStruct((BLK, WIDTH), F32)
     half_turned = jax.ShapeDtypeStruct((WIDTH, BLK), BF16)
@@ -192,14 +190,13 @@
         state_shape,
         small,
         2**19,
-        limit=60,
         in_specs=[pl.BlockSpec(memory_space=pltpu.HBM)] * 2,
         scratch_shapes=[
             pltpu.VMEM((BLK, WIDTH), BF16),
             pltpu.VMEM((BLK, WIDTH), BF16),
-            pltpu.SemaphoreType.DMA((2, CHUNKS)),
+            pltpu.SemaphoreType.DMA((2,)),
         ],
-    )(keys, values)
+    )(pltpu.with_memory_space_constraint(keys, pltpu.HBM), pltpu.with_memory_space_constraint(values, pltpu.HBM))
     key_state = carried(key_terms, before_kernel)
     inner, scaled = call(local_kernel, (full_turned, full_turned), 2 * square, 2**21)(
         queries, keys, values, gain, grad_out
@@ -215,9 +212,19 @@
     grad_q, inner_k, inner_v = call(inner_kernel, (half, full, full), 6 * square, 2**22)(
         queries, keys, values, grad_attn, key_state
     )
-    grad_k, grad_v = call(last_kernel, (half, half), 2 * small, 2**21)(
-        keys, values, inner_k, inner_v, grad_state
-    )
+    grad_k, grad_v = call(
+        last_kernel,
+        (half, half),
+        2 * small,
+        2**21,
+        in_specs=[pl.BlockSpec(memory_space=pltpu.VMEM)] * 5,
+        out_specs=(pl.BlockSpec(memory_space=pltpu.HBM),) * 2,
+        scratch_shapes=[
+            pltpu.VMEM((BLK, WIDTH), BF16),
+            pltpu.VMEM((BLK, WIDTH), BF16),
+            pltpu.SemaphoreType.DMA((2, BLK // TILE)),
+        ],
+    )(keys, values, inner_k, inner_v, grad_state)
     return grad_q, grad_k, grad_v
 
 

time: 86.9 us -> 85.9 us (0.988)
  no operation moved by 1% of the time
where the time goes in v3:
time: 85.9 us; the launch traced here: 85.2 us
  blocking collectives  51.5 us (60%)
  waiting for transfers between devices  14.6 us (17%)
  starting transfers between devices  10.8 us (13%)
  Pallas kernels  7.61 us (9%)
    all_to_all x2, blocking collectives, carried(): pieces = lax.all_to_all(total.reshape(SEQ, 8, 128), 'seq', 0, 0, tiled=True)  36.6 us
    all_to_all x1, blocking collectives, local(): sums = lax.all_to_all(sums, 'tp', 0, 0, tiled=True)  14.9 us
    all_to_all x2, waiting for transfers between devices, carried(): back = lax.all_to_all(sums, 'seq', 0, 0, tiled=True)  14.6 us
    all_to_all x2, starting transfers between devices, carried(): back = lax.all_to_all(sums, 'seq', 0, 0, tiled=True)  10.8 us
    pallas_call x1, Pallas kernels, local(): call(inner_kernel, (half, full, full), 6 * square, 2 ** 22)  2.38 us
  transfers between devices with their start and end apart: 2, of which 2 were waited for; matrix products, arithmetic and copies ran while one was open for 0% of the time, Pallas kernels for 4%

profile of v3, /device:TPU:6, one launch (start us, length us, event | category | flops | bytes accessed | tf_op | source)
XLA Modules:
  0.0 85.2 jit_solution(3639545904370084443)
XLA Ops:
  0.6 0.0 copy-start.3
  0.6 1.4 %shard_map.77 = f32[256,128]{1,0:T(8,128)S(1)} custom-call(bf16[512,256]{1,0:T(8,128)(2,1)} %k_ref.5, bf16[512,256]{1,0:T(8,128)(2,1)} %v_ref.5), custom_call_target="tpu_custom_call" | custom-call | flops 33554432 | bytes 524288 | tf_op jit(solution)/shard_map/pallas_call | solution.py:188
  2.0 0.0 copy-start.4
  2.0 0.0 copy-start.2
  2.0 22.3 %all_to_all.25.in_ref = f32[32,8,128]{2,1,0:T(8,128)S(1)} all-to-all(f32[32,8,128]{2,1,0:T(8,128)S(1)} %bitcast.4), channel_id=1, replica_groups=mesh['seq'=32,'tp'=16] {'seq'}, dimensions={0} | all-to-all | bytes 262144 | tf_op jit(solution)/shard_map/all_to_all | solution.py:173
  24.3 0.0 copy-start
  24.3 0.0 copy-start.1
  24.3 0.7 shard_map.78
  25.0 5.3 %all-to-all-start.1 = ((f32[32,8,128]{2,1,0:T(8,128)}), f32[32,8,128]{2,1,0:T(8,128)S(1)}, u32[]{:S(2)}, u32[]{:S(2)}) async-start(f32[32,8,128]{2,1,0:T(8,128)} %shard_map.78), calls=%async_computation.1 | async-start | bytes 262144 | tf_op jit(solution)/shard_map/all_to_all | solution.py:175
  30.3 0.0 copy-done.4
  30.3 0.0 copy-done.3
  30.3 0.0 copy-done.2
  30.3 0.0 copy-done
  30.3 0.0 copy-done.1
  30.4 0.9 %shard_map.76 = (f32[256,512]{1,0:T(8,128)S(1)}, f32[256,512]{1,0:T(8,128)S(1)}) custom-call(bf16[512,256]{1,0:T(8,128)(2,1)S(1)} %copy-done.2, bf16[512,256]{1,0:T(8,128)(2,1)S(1)} %copy-done, bf16[512,256]{1,0:T(8,128)(2,1)S(1)} %copy-done.1, bf16[1,256]{1,0:T(2,128)(2,1)S(1)} %reshape.21.gain_ref, bf16[512,256]{1,0:T(8,128)(2,1)S(1)} %copy-done.3), custom_call_target="tpu_custom_call" | custom-call | flops 268435456 | bytes 2097152 | tf_op jit(solution)/shard_map/pallas_call | solution.py:201
  31.3 8.0 %all-to-all-done.1 = f32[32,8,128]{2,1,0:T(8,128)S(1)} async-done(((f32[32,8,128]{2,1,0:T(8,128)}), f32[32,8,128]{2,1,0:T(8,128)S(1)}, u32[]{:S(2)}, u32[]{:S(2)}) %all-to-all-start.1) | async-done | bytes 131104 | tf_op jit(solution)/shard_map/all_to_all | solution.py:175
  39.3 0.3 shard_map.79
  39.6 14.9 %all_to_all.26.sums_ref = f32[16,8,128]{2,1,0:T(8,128)S(1)} all-to-all(f32[16,8,128]{2,1,0:T(8,128)S(1)} %get-tuple-element.17), channel_id=1, replica_groups=mesh['seq'=32,'tp'=16] {'tp'}, dimensions={0} | all-to-all | bytes 131072 | tf_op jit(solution)/shard_map/all_to_all | solution.py:207
  54.4 0.2 shard_map.80
  54.7 14.3 %all_to_all.27.in_ref = f32[32,8,128]{2,1,0:T(8,128)S(1)} all-to-all(f32[32,8,128]{2,1,0:T(8,128)S(1)} %bitcast.8), channel_id=1, replica_groups=mesh['seq'=32,'tp'=16] {'seq'}, dimensions={0} | all-to-all | bytes 262144 | tf_op jit(solution)/shard_map/all_to_all | solution.py:173
  69.0 0.7 shard_map.82
  69.7 5.5 %all-to-all-start.4 = ((f32[32,8,128]{2,1,0:T(8,128)}), f32[32,8,128]{2,1,0:T(8,128)S(1)}, u32[]{:S(2)}, u32[]{:S(2)}) async-start(f32[32,8,128]{2,1,0:T(8,128)} %shard_map.82), calls=%async_computation.4 | async-start | bytes 262144 | tf_op jit(solution)/shard_map/all_to_all | solution.py:175
  75.2 2.4 %shard_map.81 = (bf16[512,256]{1,0:T(8,128)(2,1)}, f32[512,256]{1,0:T(8,128)S(1)}, f32[512,256]{1,0:T(8,128)S(1)}) custom-call(bf16[512,256]{1,0:T(8,128)(2,1)S(1)} %copy-done.2, bf16[512,256]{1,0:T(8,128)(2,1)S(1)} %copy-done, bf16[512,256]{1,0:T(8,128)(2,1)S(1)} %copy-done.1, bf16[256,512]{1,0:T(8,128)(2,1)S(1)} %get-tuple-element.18.g_ref, ...), custom_call_target="tpu_custom_call" | custom-call | flops 805306368 | bytes 4194304 | tf_op jit(solution)/shard_map/pallas_call | solution.py:212
  77.6 6.6 %all-to-all-done.4 = f32[32,8,128]{2,1,0:T(8,128)S(1)} async-done(((f32[32,8,128]{2,1,0:T(8,128)}), f32[32,8,128]{2,1,0:T(8,128)S(1)}, u32[]{:S(2)}, u32[]{:S(2)}) %all-to-all-start.4) | async-done | bytes 131104 | tf_op jit(solution)/shard_map/all_to_all | solution.py:175
  84.2 1.0 %shard_map.83 = (bf16[512,256]{1,0:T(8,128)(2,1)}, bf16[512,256]{1,0:T(8,128)(2,1)}) custom-call(bf16[512,256]{1,0:T(8,128)(2,1)S(1)} %copy-done, bf16[512,256]{1,0:T(8,128)(2,1)S(1)} %copy-done.1, f32[512,256]{1,0:T(8,128)S(1)} %get-tuple-element.20.gk_in_ref, f32[512,256]{1,0:T(8,128)S(1)} %get-tuple-element.21.gv_in_ref, f32[256,128]{1,0:T(8,128)S(1)} %bitcast.7), custom_call_target="tpu_custom_call" | custom-call | flops 67108864 | bytes 2097152 | tf_op jit(solution)/shard_map/pallas_call | solution.py:215
  (1 shorter events, 0.0 us)
Async XLA Ops:
  0.6 29.7 %copy-start.3 = (bf16[512,256]{1,0:T(8,128)(2,1)S(1)}, bf16[512,256]{1,0:T(8,128)(2,1)}, u32[]{:S(2)}) copy-start(bf16[512,256]{1,0:T(8,128)(2,1)} %go_ref.1) | copy-start | bytes 786436
  2.0 28.3 %copy-start.4 = (bf16[256]{0:T(256)(128)(2,1)S(1)}, bf16[256]{0:T(256)(128)(2,1)}, u32[]{:S(2)}) copy-start(bf16[256]{0:T(256)(128)(2,1)} %param.8) | copy-start | bytes 1540
  2.0 28.3 %copy-start.2 = (bf16[512,256]{1,0:T(8,128)(2,1)S(1)}, bf16[512,256]{1,0:T(8,128)(2,1)}, u32[]{:S(2)}) copy-start(bf16[512,256]{1,0:T(8,128)(2,1)} %q_ref.7) | copy-start | bytes 786436
  24.3 6.0 %copy-start = (bf16[512,256]{1,0:T(8,128)(2,1)S(1)}, bf16[512,256]{1,0:T(8,128)(2,1)}, u32[]{:S(2)}) copy-start(bf16[512,256]{1,0:T(8,128)(2,1)} %k_ref.5) | copy-start | bytes 786436
  24.3 6.0 %copy-start.1 = (bf16[512,256]{1,0:T(8,128)(2,1)S(1)}, bf16[512,256]{1,0:T(8,128)(2,1)}, u32[]{:S(2)}) copy-start(bf16[512,256]{1,0:T(8,128)(2,1)} %v_ref.5) | copy-start | bytes 786436
  25.0 14.3 %all-to-all-start.1 = ((f32[32,8,128]{2,1,0:T(8,128)}), f32[32,8,128]{2,1,0:T(8,128)S(1)}, u32[]{:S(2)}, u32[]{:S(2)}) async-start(f32[32,8,128]{2,1,0:T(8,128)} %shard_map.78), calls=%async_computation.1 | async-start | bytes 262144 | tf_op jit(solution)/shard_map/all_to_all | solution.py:175
  69.7 14.5 %all-to-all-start.4 = ((f32[32,8,128]{2,1,0:T(8,128)}), f32[32,8,128]{2,1,0:T(8,128)S(1)}, u32[]{:S(2)}, u32[]{:S(2)}) async-start(f32[32,8,128]{2,1,0:T(8,128)} %shard_map.82), calls=%async_computation.4 | async-start | bytes 262144 | tf_op jit(solution)/shard_map/all_to_all | solution.py:175

commit v4 on v3

--- a/solution.py
+++ b/solution.py
@@ -1,3 +1,5 @@
+import functools
+
 import jax
 import jax.numpy as jnp
 from jax import lax
@@ -14,6 +16,9 @@
 SEQ = 32
 TP = 16
 EPSILON = 1e-06
+FIRST_BEFORE = 5 * 4 + 2
+FIRST_AFTER = 4 * 4 + 2
+FIRST_TP = 4 * 2 + 1
 
 F32 = jnp.float32
 BF16 = jnp.bfloat16
@@ -55,10 +60,11 @@
     )
 
 
-def state_kernel(k_hbm, v_hbm, out_ref, k_ref, v_ref, sems):
+def state_kernel(k_hbm, v_hbm, gain_hbm, out_ref, gain_ref, k_ref, v_ref, sems):
     copies = (
         pltpu.make_async_copy(k_hbm, k_ref, sems.at[0]),
         pltpu.make_async_copy(v_hbm, v_ref, sems.at[1]),
+        pltpu.make_async_copy(gain_hbm, gain_ref, sems.at[2]),
     )
     for copy in copies:
         copy.start()
@@ -68,46 +74,50 @@
         out_ref[head(h), :] = tn(v_ref[:, head(h)], k_ref[:, head(h)])
 
 
-def before_kernel(in_ref, out_ref):
+def slot(block, first):
+    return (block - first) % SEQ
+
+
+def before_kernel(first, in_ref, out_ref):
     acc = jnp.zeros((8, 128), F32)
     for b in range(SEQ):
-        out_ref[b] = acc
-        acc = acc + in_ref[b]
-
-
-def after_kernel(in_ref, out_ref):
+        out_ref[slot(b, first)] = acc
+        acc = acc + in_ref[slot(b, first)]
+
+
+def after_kernel(first, in_ref, out_ref):
     acc = jnp.zeros((8, 128), F32)
     for b in reversed(range(SEQ)):
-        out_ref[b] = acc
-        acc = acc + in_ref[b]
-
-
-def local_kernel(q_ref, k_ref, v_ref, gain_ref, go_ref, inner_ref, scaled_ref):
-    lower, _ = masks()
-    scaled_ref[...] = (go_ref[...].astype(F32) * gain_ref[...].astype(F32)).T
-    for h in range(HEADS):
+        out_ref[slot(b, first)] = acc
+        acc = acc + in_ref[slot(b, first)]
+
+
+def attn_kernel(q_ref, k_ref, v_ref, gain_ref, go_ref, state_ref, attn_ref, scaled_ref, sums_ref):
+    _, upper = masks()
+    gain = jnp.broadcast_to(gain_ref[...].astype(F32)[None, :], (8, WIDTH)).T[:, 0:1]
+    square = [jnp.zeros((8, TILE), F32) for _ in range(BLK // TILE)]
+    cross = [jnp.zeros((8, TILE), F32) for _ in range(BLK // TILE)]
+    for h in range(HEADS):
+        state = state_ref[head(h), :].astype(BF16)
+        v = v_ref[:, head(h)].T
+        scaled_ref[head(h), :] = go_ref[:, head(h)].T.astype(F32) * gain[head(h)]
         for t in range(BLK // TILE):
-            attn = None
+            q = q_ref[tile(t), head(h)]
+            attn = nt(state, q)
             for s in range(t + 1):
-                scores = nt(q_ref[tile(t), head(h)], k_ref[tile(s), head(h)])
+                scores = nt(k_ref[tile(s), head(h)], q)
                 if s == t:
-                    scores = jnp.where(lower, scores, 0.0)
-                term = nn(scores.astype(BF16), v_ref[tile(s), head(h)])
-                attn = term if attn is None else attn + term
-            inner_ref[head(h), tile(t)] = attn.T
-
-
-def attn_kernel(q_ref, inner_ref, scaled_ref, state_ref, attn_ref, sums_ref):
-    square = jnp.zeros((8, BLK), F32)
-    cross = jnp.zeros((8, BLK), F32)
-    for h in range(HEADS):
-        attn = inner_ref[head(h), :] + nt(state_ref[head(h), :].astype(BF16), q_ref[:, head(h)])
-        attn_ref[head(h), :] = attn
-        square = square + jnp.sum((attn * attn).reshape(HD // 8, 8, BLK), axis=0)
-        cross = cross + jnp.sum((scaled_ref[head(h), :] * attn).reshape(HD // 8, 8, BLK), axis=0)
-    square = jnp.sum(square, axis=0, keepdims=True)
-    cross = jnp.sum(cross, axis=0, keepdims=True)
-    rows = [x[:, i * 128 : (i + 1) * 128] for x in (square, cross) for i in range(BLK // 128)]
+                    scores = jnp.where(upper, scores, 0.0)
+                attn = attn + nn(v[:, tile(s)], scores.astype(BF16))
+            attn_ref[head(h), tile(t)] = attn
+            scaled = scaled_ref[head(h), tile(t)]
+            square[t] = square[t] + jnp.sum((attn * attn).reshape(HD // 8, 8, TILE), axis=0)
+            cross[t] = cross[t] + jnp.sum((scaled * attn).reshape(HD // 8, 8, TILE), axis=0)
+    rows = []
+    for kind in (square, cross):
+        for part in kind:
+            row = jnp.sum(part, axis=0, keepdims=True)
+            rows += [row[:, i * 128 : (i + 1) * 128] for i in range(TILE // 128)]
     sums_ref[...] = jnp.broadcast_to(jnp.concatenate(rows, axis=0)[None], (TP, 8, 128))
 
 
@@ -169,15 +179,23 @@
         copy.wait()
 
 
-def carried(total, kernel):
-    pieces = lax.all_to_all(total.reshape(SEQ, 8, 128), "seq", 0, 0, tiled=True)
-    sums = call(kernel, pltpu.VMEM((SEQ, 8, 128), F32), 2**15, 2**18)(pieces)
-    back = lax.all_to_all(sums, "seq", 0, 0, tiled=True)
+def listed(size, first):
+    return [[(first + i) % size for i in range(size)]]
+
+
+def carried(total, kernel, first):
+    groups = listed(SEQ, first)
+    pieces = lax.all_to_all(
+        total.reshape(SEQ, 8, 128), "seq", 0, 0, tiled=True, axis_index_groups=groups
+    )
+    sums = call(
+        functools.partial(kernel, first), pltpu.VMEM((SEQ, 8, 128), F32), 2**15, 2**18
+    )(pieces)
+    back = lax.all_to_all(sums, "seq", 0, 0, tiled=True, axis_index_groups=groups)
     return back.reshape(WIDTH, HD)
 
 
 def local(queries, keys, values, gain, grad_out):
-    gain = gain.reshape(1, WIDTH)
     state_shape = pltpu.VMEM((WIDTH, HD), F32)
     half = jax.ShapeDtypeStruct((BLK, WIDTH), BF16)
     full = jax.ShapeDtypeStruct((BLK, WIDTH), F32)
@@ -185,30 +203,35 @@
     full_turned = jax.ShapeDtypeStruct((WIDTH, BLK), F32)
     small = 2 * HEADS * BLK * HD * HD
     square = 2 * HEADS * BLK * BLK * HD
-    key_terms = call(
+    keys_here, values_here, gain_here = (
+        pltpu.with_memory_space_constraint(x, pltpu.HBM) for x in (keys, values, gain)
+    )
+    key_terms, gain = call(
         state_kernel,
-        state_shape,
+        (state_shape, pltpu.VMEM((WIDTH,), BF16)),
         small,
         2**19,
-        in_specs=[pl.BlockSpec(memory_space=pltpu.HBM)] * 2,
+        in_specs=[pl.BlockSpec(memory_space=pltpu.HBM)] * 3,
         scratch_shapes=[
             pltpu.VMEM((BLK, WIDTH), BF16),
             pltpu.VMEM((BLK, WIDTH), BF16),
-            pltpu.SemaphoreType.DMA((2,)),
+            pltpu.SemaphoreType.DMA((3,)),
         ],
-    )(pltpu.with_memory_space_constraint(keys, pltpu.HBM), pltpu.with_memory_space_constraint(values, pltpu.HBM))
-    key_state = carried(key_terms, before_kernel)
-    inner, scaled = call(local_kernel, (full_turned, full_turned), 2 * square, 2**21)(
-        queries, keys, values, gain, grad_out
-    )
-    attn, sums = call(
-        attn_kernel, (full_turned, jax.ShapeDtypeStruct((TP, 8, 128), F32)), small, 2**21
-    )(queries, inner, scaled, key_state)
-    sums = lax.all_to_all(sums, "tp", 0, 0, tiled=True)
+    )(keys_here, values_here, gain_here)
+    key_state = carried(key_terms, before_kernel, FIRST_BEFORE)
+    attn, scaled, sums = call(
+        attn_kernel,
+        (full_turned, full_turned, jax.ShapeDtypeStruct((TP, 8, 128), F32)),
+        small + 2 * square,
+        2**21,
+    )(queries, keys, values, gain, grad_out, key_state)
+    sums = lax.all_to_all(
+        sums, "tp", 0, 0, tiled=True, axis_index_groups=listed(TP, FIRST_TP)
+    )
     grad_attn, query_terms = call(grad_kernel, (half_turned, state_shape), small, 2**21)(
         queries, scaled, attn, sums
     )
-    grad_state = carried(query_terms, after_kernel)
+    grad_state = carried(query_terms, after_kernel, FIRST_AFTER)
     grad_q, inner_k, inner_v = call(inner_kernel, (half, full, full), 6 * square, 2**22)(
         queries, keys, values, grad_attn, key_state
     )

time: 85.9 us -> 78.3 us (0.912)
  waiting for transfers between devices: 14.6 us -> 3.03 us
  blocking collectives: 51.5 us -> 58.2 us
  starting transfers between devices: 10.8 us -> 9.07 us
  Pallas kernels: 7.61 us -> 6.65 us
    all_to_all x2 -> x1, waiting for transfers between devices: 14.6 us -> 3.03 us  [carried(): lax.all_to_all(sums, 'seq', 0, 0, tiled=True, axis_index_groups=groups)]
    all_to_all x3 -> x4, blocking collectives: 51.5 us -> 58.2 us  [the longest x2 33.7 us: carried(): lax.all_to_all(total.reshape(SEQ, 8, 128), 'seq', 0, 0, tiled=True, axis_...]
    all_to_all x2 -> x1, starting transfers between devices: 10.8 us -> 9.07 us  [carried(): lax.all_to_all(sums, 'seq', 0, 0, tiled=True, axis_index_groups=groups)]
    pallas_call x5 -> x4, Pallas kernels: 3.95 us -> 2.99 us  [the longest x1 1.38 us: local(): call(state_kernel, (state_shape, pltpu.VMEM((WIDTH,), BF16)), small, 2 **...]
  transfers between devices with their start and end apart: 2 -> 1, of which waited for: 2 -> 1; matrix products, arithmetic and copies ran while one was open for 0% -> 0% of each run, Pallas kernels for 4% -> 3%
where the time goes in v4:
time: 78.3 us; the launch traced here: 77.7 us
  blocking collectives  58.2 us (74%)
  starting transfers between devices  9.07 us (12%)
  Pallas kernels  6.65 us (8%)
  waiting for transfers between devices  3.03 us (4%)
    all_to_all x2, blocking collectives, carried(): lax.all_to_all(total.reshape(SEQ, 8, 128), 'seq', 0, 0, tiled=True, axis_...  33.7 us
    all_to_all x1, blocking collectives, carried(): lax.all_to_all(sums, 'seq', 0, 0, tiled=True, axis_index_groups=groups)  13.9 us
    all_to_all x1, blocking collectives, local(): lax.all_to_all(sums, 'tp', 0, 0, tiled=True, axis_index_groups=listed(TP,...  10.6 us
    all_to_all x1, starting transfers between devices, carried(): lax.all_to_all(sums, 'seq', 0, 0, tiled=True, axis_index_groups=groups)  9.07 us
    all_to_all x1, waiting for transfers between devices, carried(): lax.all_to_all(sums, 'seq', 0, 0, tiled=True, axis_index_groups=groups)  3.03 us
    pallas_call x1, Pallas kernels, local(): call(inner_kernel, (half, full, full), 6 * square, 2 ** 22)  2.38 us
  transfers between devices with their start and end apart: 1, of which 1 were waited for; matrix products, arithmetic and copies ran while one was open for 0% of the time, Pallas kernels for 3%

profile of v4, /device:TPU:6, one launch (start us, length us, event | category | flops | bytes accessed | tf_op | source)
XLA Modules:
  0.0 77.7 jit_solution(8294320262147654683)
XLA Ops:
  0.6 0.0 copy-start.3
  0.6 1.4 %shard_map.76 = (f32[256,128]{1,0:T(8,128)S(1)}, bf16[256]{0:T(256)(128)(2,1)S(1)}) custom-call(bf16[512,256]{1,0:T(8,128)(2,1)} %k_ref.5, bf16[512,256]{1,0:T(8,128)(2,1)} %v_ref.5, bf16[256]{0:T(256)(128)(2,1)} %gain_hbm.1), custom_call_target="tpu_custom_call" | custom-call | flops 33554432 | bytes 524288 | tf_op jit(solution)/shard_map/pallas_call | solution.py:209
  2.0 0.0 copy-start.2
  2.0 20.0 %all_to_all.25.in_ref = f32[32,8,128]{2,1,0:T(8,128)S(1)} all-to-all(f32[32,8,128]{2,1,0:T(8,128)S(1)} %bitcast.8), channel_id=1, replica_groups={{352,368,384,400,416,432,448,464,480,496,0,16,32,48,64,80,96,112,128,14..., dimensions={0} | all-to-all | bytes 262144 | tf_op jit(solution)/shard_map/all_to_all | solution.py:188
  22.0 0.0 copy-start
  22.0 0.0 copy-start.1
  22.0 13.9 %all_to_all.26 = f32[32,8,128]{2,1,0:T(8,128)S(1)} all-to-all(f32[32,8,128]{2,1,0:T(8,128)S(1)} %shard_map.77), channel_id=1, replica_groups={{352,368,384,400,416,432,448,464,480,496,0,16,32,48,64,80,96,112,128,14..., dimensions={0} | all-to-all | bytes 262144 | tf_op jit(solution)/shard_map/all_to_all | solution.py:194
  35.9 0.0 copy-done.3
  35.9 0.0 copy-done.2
  35.9 0.0 copy-done
  36.0 0.0 copy-done.1
  36.0 0.9 %shard_map.78 = (f32[256,512]{1,0:T(8,128)S(1)}, f32[256,512]{1,0:T(8,128)S(1)}, f32[16,8,128]{2,1,0:T(8,128)S(1)}) custom-call(bf16[512,256]{1,0:T(8,128)(2,1)S(1)} %copy-done.2, bf16[512,256]{1,0:T(8,128)(2,1)S(1)} %copy-done, bf16[512,256]{1,0:T(8,128)(2,1)S(1)} %copy-done.1, bf16[256]{0:T(256)(128)(2,1)S(1)} %get-tuple-element.15.gain_ref, ...), custom_call_target="tpu_custom_call" | custom-call | flops 301989888 | bytes 2097152 | tf_op jit(solution)/shard_map/pallas_call | solution.py:222
  36.9 10.6 %all_to_all.27.sums_ref = f32[16,8,128]{2,1,0:T(8,128)S(1)} all-to-all(f32[16,8,128]{2,1,0:T(8,128)S(1)} %get-tuple-element.19), channel_id=1, replica_groups={{9,10,11,12,13,14,15,0,1,2,3,4,5,6,7,8},{25,26,27,28,29,30,31,16,17,18,..., dimensions={0} | all-to-all | bytes 131072 | tf_op jit(solution)/shard_map/all_to_all | solution.py:228
  47.5 0.3 shard_map.79
  47.7 13.7 %all_to_all.28.in_ref = f32[32,8,128]{2,1,0:T(8,128)S(1)} all-to-all(f32[32,8,128]{2,1,0:T(8,128)S(1)} %bitcast.7), channel_id=1, replica_groups={{288,304,320,336,352,368,384,400,416,432,448,464,480,496,0,16,32,48,64,..., dimensions={0} | all-to-all | bytes 262144 | tf_op jit(solution)/shard_map/all_to_all | solution.py:188
  61.5 0.7 shard_map.81
  62.2 9.1 %all-to-all-start.4 = ((f32[32,8,128]{2,1,0:T(8,128)}), f32[32,8,128]{2,1,0:T(8,128)S(1)}, u32[]{:S(2)}, u32[]{:S(2)}) async-start(f32[32,8,128]{2,1,0:T(8,128)} %shard_map.81), calls=%async_computation.4 | async-start | bytes 262144 | tf_op jit(solution)/shard_map/all_to_all | solution.py:194
  71.2 2.4 %shard_map.80 = (bf16[512,256]{1,0:T(8,128)(2,1)}, f32[512,256]{1,0:T(8,128)S(1)}, f32[512,256]{1,0:T(8,128)S(1)}) custom-call(bf16[512,256]{1,0:T(8,128)(2,1)S(1)} %copy-done.2, bf16[512,256]{1,0:T(8,128)(2,1)S(1)} %copy-done, bf16[512,256]{1,0:T(8,128)(2,1)S(1)} %copy-done.1, bf16[256,512]{1,0:T(8,128)(2,1)S(1)} %get-tuple-element.20.g_ref, ...), custom_call_target="tpu_custom_call" | custom-call | flops 805306368 | bytes 4194304 | tf_op jit(solution)/shard_map/pallas_call | solution.py:235
  73.6 3.0 %all-to-all-done.4 = f32[32,8,128]{2,1,0:T(8,128)S(1)} async-done(((f32[32,8,128]{2,1,0:T(8,128)}), f32[32,8,128]{2,1,0:T(8,128)S(1)}, u32[]{:S(2)}, u32[]{:S(2)}) %all-to-all-start.4) | async-done | bytes 131104 | tf_op jit(solution)/shard_map/all_to_all | solution.py:194
  76.7 1.0 %shard_map.82 = (bf16[512,256]{1,0:T(8,128)(2,1)}, bf16[512,256]{1,0:T(8,128)(2,1)}) custom-call(bf16[512,256]{1,0:T(8,128)(2,1)S(1)} %copy-done, bf16[512,256]{1,0:T(8,128)(2,1)S(1)} %copy-done.1, f32[512,256]{1,0:T(8,128)S(1)} %get-tuple-element.22.gk_in_ref, f32[512,256]{1,0:T(8,128)S(1)} %get-tuple-element.23.gv_in_ref, f32[256,128]{1,0:T(8,128)S(1)} %bitcast.6), custom_call_target="tpu_custom_call" | custom-call | flops 67108864 | bytes 2097152 | tf_op jit(solution)/shard_map/pallas_call | solution.py:238
  (1 shorter events, 0.0 us)
Async XLA Ops:
  0.6 35.3 %copy-start.3 = (bf16[512,256]{1,0:T(8,128)(2,1)S(1)}, bf16[512,256]{1,0:T(8,128)(2,1)}, u32[]{:S(2)}) copy-start(bf16[512,256]{1,0:T(8,128)(2,1)} %go_ref.1) | copy-start | bytes 786436
  2.0 33.9 %copy-start.2 = (bf16[512,256]{1,0:T(8,128)(2,1)S(1)}, bf16[512,256]{1,0:T(8,128)(2,1)}, u32[]{:S(2)}) copy-start(bf16[512,256]{1,0:T(8,128)(2,1)} %q_ref.5) | copy-start | bytes 786436
  22.0 13.9 %copy-start = (bf16[512,256]{1,0:T(8,128)(2,1)S(1)}, bf16[512,256]{1,0:T(8,128)(2,1)}, u32[]{:S(2)}) copy-start(bf16[512,256]{1,0:T(8,128)(2,1)} %k_ref.5) | copy-start | bytes 786436
  22.0 13.9 %copy-start.1 = (bf16[512,256]{1,0:T(8,128)(2,1)S(1)}, bf16[512,256]{1,0:T(8,128)(2,1)}, u32[]{:S(2)}) copy-start(bf16[512,256]{1,0:T(8,128)(2,1)} %v_ref.5) | copy-start | bytes 786436
  62.2 14.5 %all-to-all-start.4 = ((f32[32,8,128]{2,1,0:T(8,128)}), f32[32,8,128]{2,1,0:T(8,128)S(1)}, u32[]{:S(2)}, u32[]{:S(2)}) async-start(f32[32,8,128]{2,1,0:T(8,128)} %shard_map.81), calls=%async_computation.4 | async-start | bytes 262144 | tf_op jit(solution)/shard_map/all_to_all | solution.py:194

commit v5 on v4

--- a/solution.py
+++ b/solution.py
@@ -1,5 +1,3 @@
-import functools
-
 import jax
 import jax.numpy as jnp
 from jax import lax
@@ -14,11 +12,17 @@
 HEADS = 2
 WIDTH = HEADS * HD
 SEQ = 32
+HALF = 16
+PIECE = 16
 TP = 16
 EPSILON = 1e-06
-FIRST_BEFORE = 5 * 4 + 2
-FIRST_AFTER = 4 * 4 + 2
-FIRST_TP = 4 * 2 + 1
+Z_A = 0
+Z_D = 0
+FIRST_A = 6
+FIRST_B = 22
+FIRST_TP = 9
+FIRST_C = 22
+FIRST_D = 10
 
 F32 = jnp.float32
 BF16 = jnp.bfloat16
@@ -60,6 +64,20 @@
     )
 
 
+def listed(size, first):
+    return [(first + i) % size for i in range(size)]
+
+
+def halves(z, first):
+    return [[(4 * z + half + i) % SEQ for i in listed(HALF, first)] for half in (0, HALF)]
+
+
+OWNERS_BEFORE = halves(Z_A, FIRST_A)
+BACK_BEFORE = listed(SEQ, FIRST_B)
+OUT_AFTER = listed(SEQ, FIRST_C)
+OWNERS_AFTER = halves(Z_D, FIRST_D)
+
+
 def state_kernel(k_hbm, v_hbm, gain_hbm, out_ref, gain_ref, k_ref, v_ref, sems):
     copies = (
         pltpu.make_async_copy(k_hbm, k_ref, sems.at[0]),
@@ -74,31 +92,45 @@
         out_ref[head(h), :] = tn(v_ref[:, head(h)], k_ref[:, head(h)])
 
 
-def slot(block, first):
-    return (block - first) % SEQ
-
-
-def before_kernel(first, in_ref, out_ref):
-    acc = jnp.zeros((8, 128), F32)
-    for b in range(SEQ):
-        out_ref[slot(b, first)] = acc
-        acc = acc + in_ref[slot(b, first)]
-
-
-def after_kernel(first, in_ref, out_ref):
-    acc = jnp.zeros((8, 128), F32)
-    for b in reversed(range(SEQ)):
-        out_ref[slot(b, first)] = acc
-        acc = acc + in_ref[slot(b, first)]
-
-
-def attn_kernel(q_ref, k_ref, v_ref, gain_ref, go_ref, state_ref, attn_ref, scaled_ref, sums_ref):
+def in_half(z, half):
+    place = lax.rem(lax.axis_index("seq") + (SEQ - 4 * z), SEQ)
+    return place < HALF if half == 0 else place >= HALF
+
+
+def before_kernel(in_ref, out_ref):
+    for half, owners in enumerate(OWNERS_BEFORE):
+
+        @pl.when(in_half(Z_A, half))
+        def _():
+            acc = jnp.zeros((PIECE, 128), F32)
+            for b in range(SEQ):
+                out_ref[BACK_BEFORE.index(b)] = acc
+                if b in owners:
+                    acc = acc + in_ref[owners.index(b)]
+
+
+def after_kernel(in_ref, out_ref):
+    for half, owners in enumerate(OWNERS_AFTER):
+
+        @pl.when(in_half(Z_D, half))
+        def _():
+            acc = jnp.zeros((PIECE, 128), F32)
+            for b in reversed(range(SEQ)):
+                if b in owners:
+                    out_ref[owners.index(b)] = acc
+                acc = acc + in_ref[OUT_AFTER.index(b)]
+
+
+def attn_kernel(q_ref, k_ref, v_ref, gain_ref, go_ref, parts_ref, attn_ref, scaled_ref, sums_ref, state_ref):
+    for i, pair in enumerate(zip(*OWNERS_BEFORE)):
+        part = sum(parts_ref[BACK_BEFORE.index(owner)] for owner in pair)
+        state_ref[i * PIECE : (i + 1) * PIECE, :] = part.astype(BF16)
     _, upper = masks()
     gain = jnp.broadcast_to(gain_ref[...].astype(F32)[None, :], (8, WIDTH)).T[:, 0:1]
     square = [jnp.zeros((8, TILE), F32) for _ in range(BLK // TILE)]
     cross = [jnp.zeros((8, TILE), F32) for _ in range(BLK // TILE)]
     for h in range(HEADS):
-        state = state_ref[head(h), :].astype(BF16)
+        state = state_ref[head(h), :]
         v = v_ref[:, head(h)].T
         scaled_ref[head(h), :] = go_ref[:, head(h)].T.astype(F32) * gain[head(h)]
         for t in range(BLK // TILE):
@@ -130,14 +162,18 @@
     for h in range(HEADS):
         g = (scaled_ref[head(h), :] * inv - attn_ref[head(h), :] * factor).astype(BF16)
         g_ref[head(h), :] = g
-        out_ref[head(h), :] = nn(g, q_ref[:, head(h)])
+        terms = nn(g, q_ref[:, head(h)])
+        for i in range(HD // PIECE):
+            part = terms[i * PIECE : (i + 1) * PIECE]
+            for owners in OWNERS_AFTER:
+                out_ref[OUT_AFTER.index(owners[h * (HD // PIECE) + i])] = part
 
 
 def inner_kernel(q_ref, k_ref, v_ref, g_ref, state_ref, gq_ref, gk_ref, gv_ref):
     lower, upper = masks()
     for h in range(HEADS):
         g = g_ref[head(h), :].T
-        state = state_ref[head(h), :].astype(BF16)
+        state = state_ref[head(h), :]
         for t in range(BLK // TILE):
             grad = nn(g[tile(t)], state)
             for s in range(t + 1):
@@ -179,20 +215,8 @@
         copy.wait()
 
 
-def listed(size, first):
-    return [[(first + i) % size for i in range(size)]]
-
-
-def carried(total, kernel, first):
-    groups = listed(SEQ, first)
-    pieces = lax.all_to_all(
-        total.reshape(SEQ, 8, 128), "seq", 0, 0, tiled=True, axis_index_groups=groups
-    )
-    sums = call(
-        functools.partial(kernel, first), pltpu.VMEM((SEQ, 8, 128), F32), 2**15, 2**18
-    )(pieces)
-    back = lax.all_to_all(sums, "seq", 0, 0, tiled=True, axis_index_groups=groups)
-    return back.reshape(WIDTH, HD)
+def exchange(pieces, axis, groups):
+    return lax.all_to_all(pieces, axis, 0, 0, tiled=True, axis_index_groups=groups)
 
 
 def local(queries, keys, values, gain, grad_out):
@@ -218,20 +242,29 @@
             pltpu.SemaphoreType.DMA((3,)),
         ],
     )(keys_here, values_here, gain_here)
-    key_state = carried(key_terms, before_kernel, FIRST_BEFORE)
-    attn, scaled, sums = call(
+    pieces = exchange(key_terms.reshape(HALF, PIECE, HD), "seq", OWNERS_BEFORE)
+    pieces = call(before_kernel, pltpu.VMEM((SEQ, PIECE, HD), F32), 2**16, 2**19)(pieces)
+    key_parts = exchange(pieces, "seq", [BACK_BEFORE])
+    attn, scaled, sums, key_state = call(
         attn_kernel,
-        (full_turned, full_turned, jax.ShapeDtypeStruct((TP, 8, 128), F32)),
+        (
+            full_turned,
+            full_turned,
+            jax.ShapeDtypeStruct((TP, 8, 128), F32),
+            jax.ShapeDtypeStruct((WIDTH, HD), BF16),
+        ),
         small + 2 * square,
         2**21,
-    )(queries, keys, values, gain, grad_out, key_state)
-    sums = lax.all_to_all(
-        sums, "tp", 0, 0, tiled=True, axis_index_groups=listed(TP, FIRST_TP)
-    )
-    grad_attn, query_terms = call(grad_kernel, (half_turned, state_shape), small, 2**21)(
+    )(queries, keys, values, gain, grad_out, key_parts)
+    sums = exchange(sums, "tp", [listed(TP, FIRST_TP)])
+    grad_attn, query_terms = call(
+        grad_kernel, (half_turned, pltpu.VMEM((SEQ, PIECE, HD), F32)), small, 2**21
+    )(
         queries, scaled, attn, sums
     )
-    grad_state = carried(query_terms, after_kernel, FIRST_AFTER)
+    pieces = exchange(query_terms, "seq", [OUT_AFTER])
+    pieces = call(after_kernel, pltpu.VMEM((HALF, PIECE, HD), F32), 2**16, 2**19)(pieces)
+    grad_state = exchange(pieces, "seq", OWNERS_AFTER).reshape(WIDTH, HD)
     grad_q, inner_k, inner_v = call(inner_kernel, (half, full, full), 6 * square, 2**22)(
         queries, keys, values, grad_attn, key_state
     )

time: 78.3 us -> 76.6 us (0.978)
  starting transfers between devices: 9.07 us -> 5.29 us
  blocking collectives: 58.2 us -> 60 us
    all_to_all x1, starting transfers between devices: 9.07 us -> 5.29 us  [exchange(): lax.all_to_all(pieces, axis, 0, 0, tiled=True, axis_index_groups=groups)]
    all_to_all x4, blocking collectives: 58.2 us -> 60 us  [exchange(): lax.all_to_all(pieces, axis, 0, 0, tiled=True, axis_index_groups=groups)]
where the time goes in v5:
time: 76.6 us; the launch traced here: 76.2 us
  blocking collectives  60 us (78%)
  Pallas kernels  6.6 us (9%)
  starting transfers between devices  5.29 us (7%)
  waiting for transfers between devices  3.59 us (5%)
    all_to_all x4, blocking collectives, exchange(): lax.all_to_all(pieces, axis, 0, 0, tiled=True, axis_index_groups=groups)  60 us
    all_to_all x1, starting transfers between devices, exchange(): lax.all_to_all(pieces, axis, 0, 0, tiled=True, axis_index_groups=groups)  5.29 us
    all_to_all x1, waiting for transfers between devices, exchange(): lax.all_to_all(pieces, axis, 0, 0, tiled=True, axis_index_groups=groups)  3.59 us
    pallas_call x1, Pallas kernels, local(): call(inner_kernel, (half, full, full), 6 * square, 2 ** 22)  2.37 us
  transfers between devices with their start and end apart: 1, of which 1 were waited for; matrix products, arithmetic and copies ran while one was open for 0% of the time, Pallas kernels for 3%

profile of v5, /device:TPU:6, one launch (start us, length us, event | category | flops | bytes accessed | tf_op | source)
XLA Modules:
  0.0 76.2 jit_solution(608184840258515858)
XLA Ops:
  0.6 1.3 %shard_map.76 = (f32[256,128]{1,0:T(8,128)S(1)}, bf16[256]{0:T(256)(128)(2,1)S(1)}) custom-call(bf16[512,256]{1,0:T(8,128)(2,1)} %k_ref.5, bf16[512,256]{1,0:T(8,128)(2,1)} %v_ref.5, bf16[256]{0:T(256)(128)(2,1)} %gain_hbm.1), custom_call_target="tpu_custom_call" | custom-call | flops 33554432 | bytes 524288 | tf_op jit(solution)/shard_map/pallas_call | solution.py:233
  2.0 0.0 copy-start.3
  2.0 15.7 %all_to_all.25.in_ref = f32[16,16,128]{2,1,0:T(8,128)S(1)} all-to-all(f32[16,16,128]{2,1,0:T(8,128)S(1)} %bitcast.3), channel_id=1, replica_groups={{96,112,128,144,160,176,192,208,224,240,0,16,32,48,64,80},{352,368,384,..., dimensions={0} | all-to-all | bytes 262144 | tf_op jit(solution)/shard_map/all_to_all | solution.py:219
  17.7 0.0 copy-start.2
  17.8 0.0 copy-start
  17.8 0.0 copy-start.1
  17.8 17.0 %all_to_all.26.parts_ref = f32[32,16,128]{2,1,0:T(8,128)S(1)} all-to-all(f32[32,16,128]{2,1,0:T(8,128)S(1)} %shard_map.77), channel_id=1, replica_groups={{352,368,384,400,416,432,448,464,480,496,0,16,32,48,64,80,96,112,128,14..., dimensions={0} | all-to-all | bytes 524288 | tf_op jit(solution)/shard_map/all_to_all | solution.py:219
  34.8 0.0 copy-done.3
  34.8 0.0 copy-done.2
  34.8 0.0 copy-done
  34.8 0.0 copy-done.1
  34.8 0.9 %shard_map.78 = (f32[256,512]{1,0:T(8,128)S(1)}, f32[256,512]{1,0:T(8,128)S(1)}, f32[16,8,128]{2,1,0:T(8,128)S(1)}, bf16[256,128]{1,0:T(8,128)(2,1)S(1)}) custom-call(bf16[512,256]{1,0:T(8,128)(2,1)S(1)} %copy-done.2, bf16[512,256]{1,0:T(8,128)(2,1)S(1)} %copy-done, bf16[512,256]{1,0:T(8,128)(2,1)S(1)} %copy-done.1, ...), custom_call_target="tpu_custom_call" | custom-call | flops 301989888 | bytes 2097152 | tf_op jit(solution)/shard_map/pallas_call | solution.py:248
  35.7 10.6 %all_to_all.27.sums_ref = f32[16,8,128]{2,1,0:T(8,128)S(1)} all-to-all(f32[16,8,128]{2,1,0:T(8,128)S(1)} %get-tuple-element.20), channel_id=1, replica_groups={{9,10,11,12,13,14,15,0,1,2,3,4,5,6,7,8},{25,26,27,28,29,30,31,16,17,18,..., dimensions={0} | all-to-all | bytes 131072 | tf_op jit(solution)/shard_map/all_to_all | solution.py:219
  46.3 0.3 shard_map.79
  46.6 16.7 %all_to_all.28.in_ref = f32[32,16,128]{2,1,0:T(8,128)S(1)} all-to-all(f32[32,16,128]{2,1,0:T(8,128)S(1)} %get-tuple-element.26), channel_id=1, replica_groups={{352,368,384,400,416,432,448,464,480,496,0,16,32,48,64,80,96,112,128,14..., dimensions={0} | all-to-all | bytes 524288 | tf_op jit(solution)/shard_map/all_to_all | solution.py:219
  63.2 0.7 shard_map.81
  63.9 5.3 %all-to-all-start.4 = ((f32[16,16,128]{2,1,0:T(8,128)}), f32[16,16,128]{2,1,0:T(8,128)S(1)}, u32[]{:S(2)}, u32[]{:S(2)}) async-start(f32[16,16,128]{2,1,0:T(8,128)} %shard_map.81), calls=%async_computation.4 | async-start | bytes 262144 | tf_op jit(solution)/shard_map/all_to_all | solution.py:219
  69.2 2.4 %shard_map.80 = (bf16[512,256]{1,0:T(8,128)(2,1)}, f32[512,256]{1,0:T(8,128)S(1)}, f32[512,256]{1,0:T(8,128)S(1)}) custom-call(bf16[512,256]{1,0:T(8,128)(2,1)S(1)} %copy-done.2, bf16[512,256]{1,0:T(8,128)(2,1)S(1)} %copy-done, bf16[512,256]{1,0:T(8,128)(2,1)S(1)} %copy-done.1, bf16[256,512]{1,0:T(8,128)(2,1)S(1)} %get-tuple-element.21.g_ref, ...), custom_call_target="tpu_custom_call" | custom-call | flops 805306368 | bytes 4194304 | tf_op jit(solution)/shard_map/pallas_call | solution.py:268
  71.6 3.6 %all-to-all-done.4 = f32[16,16,128]{2,1,0:T(8,128)S(1)} async-done(((f32[16,16,128]{2,1,0:T(8,128)}), f32[16,16,128]{2,1,0:T(8,128)S(1)}, u32[]{:S(2)}, u32[]{:S(2)}) %all-to-all-start.4) | async-done | bytes 131104 | tf_op jit(solution)/shard_map/all_to_all | solution.py:219
  75.2 1.0 %shard_map.82 = (bf16[512,256]{1,0:T(8,128)(2,1)}, bf16[512,256]{1,0:T(8,128)(2,1)}) custom-call(bf16[512,256]{1,0:T(8,128)(2,1)S(1)} %copy-done, bf16[512,256]{1,0:T(8,128)(2,1)S(1)} %copy-done.1, f32[512,256]{1,0:T(8,128)S(1)} %get-tuple-element.24.gk_in_ref, f32[512,256]{1,0:T(8,128)S(1)} %get-tuple-element.25.gv_in_ref, f32[256,128]{1,0:T(8,128)S(1)} %bitcast.2), custom_call_target="tpu_custom_call" | custom-call | flops 67108864 | bytes 2097152 | tf_op jit(solution)/shard_map/pallas_call | solution.py:271
  (1 shorter events, 0.0 us)
Async XLA Ops:
  2.0 32.8 %copy-start.3 = (bf16[512,256]{1,0:T(8,128)(2,1)S(1)}, bf16[512,256]{1,0:T(8,128)(2,1)}, u32[]{:S(2)}) copy-start(bf16[512,256]{1,0:T(8,128)(2,1)} %go_ref.1) | copy-start | bytes 786436
  17.7 17.1 %copy-start.2 = (bf16[512,256]{1,0:T(8,128)(2,1)S(1)}, bf16[512,256]{1,0:T(8,128)(2,1)}, u32[]{:S(2)}) copy-start(bf16[512,256]{1,0:T(8,128)(2,1)} %q_ref.5) | copy-start | bytes 786436
  17.8 17.0 %copy-start = (bf16[512,256]{1,0:T(8,128)(2,1)S(1)}, bf16[512,256]{1,0:T(8,128)(2,1)}, u32[]{:S(2)}) copy-start(bf16[512,256]{1,0:T(8,128)(2,1)} %k_ref.5) | copy-start | bytes 786436
  17.8 17.0 %copy-start.1 = (bf16[512,256]{1,0:T(8,128)(2,1)S(1)}, bf16[512,256]{1,0:T(8,128)(2,1)}, u32[]{:S(2)}) copy-start(bf16[512,256]{1,0:T(8,128)(2,1)} %v_ref.5) | copy-start | bytes 786436
  63.9 11.3 %all-to-all-start.4 = ((f32[16,16,128]{2,1,0:T(8,128)}), f32[16,16,128]{2,1,0:T(8,128)S(1)}, u32[]{:S(2)}, u32[]{:S(2)}) async-start(f32[16,16,128]{2,1,0:T(8,128)} %shard_map.81), calls=%async_computation.4 | async-start | bytes 262144 | tf_op jit(solution)/shard_map/all_to_all | solution.py:219

commit v6 on v5

--- a/solution.py
+++ b/solution.py
@@ -13,16 +13,23 @@
 WIDTH = HEADS * HD
 SEQ = 32
 HALF = 16
-PIECE = 16
+PIECE = 32
+PIECES = WIDTH // PIECE
 TP = 16
 EPSILON = 1e-06
+LAST_TILES = 2
 Z_A = 0
-Z_D = 0
+Z_B = 2
+Z_C = 0
+Z_D = 2
 FIRST_A = 6
-FIRST_B = 22
+TURN_B = 8
+TURN_C = 0
+TURN_D = 0
+FIRST_B = 10
 FIRST_TP = 9
-FIRST_C = 22
-FIRST_D = 10
+FIRST_C = 10
+FIRST_D = 6
 
 F32 = jnp.float32
 BF16 = jnp.bfloat16
@@ -68,63 +75,83 @@
     return [(first + i) % size for i in range(size)]
 
 
-def halves(z, first):
-    return [[(4 * z + half + i) % SEQ for i in listed(HALF, first)] for half in (0, HALF)]
-
-
-OWNERS_BEFORE = halves(Z_A, FIRST_A)
-BACK_BEFORE = listed(SEQ, FIRST_B)
-OUT_AFTER = listed(SEQ, FIRST_C)
-OWNERS_AFTER = halves(Z_D, FIRST_D)
+def halves(z, first, turn=0):
+    return [
+        [(4 * z + half + i) % SEQ for i in listed(HALF, first + (turn if half else 0))]
+        for half in (0, HALF)
+    ]
+
+
+OUT_BEFORE = halves(Z_A, FIRST_A)
+BACK_BEFORE = halves(Z_B, FIRST_B, TURN_B)
+OUT_AFTER = halves(Z_C, FIRST_C, TURN_C)
+BACK_AFTER = halves(Z_D, FIRST_D, TURN_D)
+
+
+def piece(block):
+    return block % PIECES
+
+
+def places(lists, p):
+    return [i for i, block in enumerate(lists[0]) if piece(block) == p]
+
+
+def own(lists, block):
+    return lists[0] if block in lists[0] else lists[1]
+
+
+def spread(terms, h, lists, out_ref):
+    for i in range(HD // PIECE):
+        for place in places(lists, h * (HD // PIECE) + i):
+            out_ref[place] = terms[i * PIECE : (i + 1) * PIECE]
+
+
+def joined(parts_ref, p, lists):
+    first, second = places(lists, p)
+    return parts_ref[first] + parts_ref[second]
 
 
 def state_kernel(k_hbm, v_hbm, gain_hbm, out_ref, gain_ref, k_ref, v_ref, sems):
     copies = (
-        pltpu.make_async_copy(k_hbm, k_ref, sems.at[0]),
-        pltpu.make_async_copy(v_hbm, v_ref, sems.at[1]),
+        pltpu.make_async_copy(v_hbm, v_ref, sems.at[0]),
+        pltpu.make_async_copy(k_hbm, k_ref, sems.at[1]),
         pltpu.make_async_copy(gain_hbm, gain_ref, sems.at[2]),
     )
     for copy in copies:
         copy.start()
-    for copy in copies:
-        copy.wait()
+    copies[0].wait()
+    turned = [v_ref[:, head(h)].T for h in range(HEADS)]
+    copies[1].wait()
     for h in range(HEADS):
-        out_ref[head(h), :] = tn(v_ref[:, head(h)], k_ref[:, head(h)])
-
-
-def in_half(z, half):
-    place = lax.rem(lax.axis_index("seq") + (SEQ - 4 * z), SEQ)
-    return place < HALF if half == 0 else place >= HALF
+        spread(nn(turned[h], k_ref[:, head(h)]), h, OUT_BEFORE, out_ref)
+    copies[2].wait()
+
+
+def running_sums(blocks, out, back, in_ref, out_ref):
+    for pair in range(SEQ // PIECES):
+
+        @pl.when(lax.div(lax.axis_index("seq"), PIECES) == pair)
+        def _():
+            senders, receivers = own(out, pair * PIECES), own(back, pair * PIECES)
+            acc = jnp.zeros((PIECE, 128), F32)
+            for b in blocks:
+                if b in receivers:
+                    out_ref[receivers.index(b)] = acc
+                if b in senders:
+                    acc = acc + in_ref[senders.index(b)]
 
 
 def before_kernel(in_ref, out_ref):
-    for half, owners in enumerate(OWNERS_BEFORE):
-
-        @pl.when(in_half(Z_A, half))
-        def _():
-            acc = jnp.zeros((PIECE, 128), F32)
-            for b in range(SEQ):
-                out_ref[BACK_BEFORE.index(b)] = acc
-                if b in owners:
-                    acc = acc + in_ref[owners.index(b)]
+    running_sums(range(SEQ), OUT_BEFORE, BACK_BEFORE, in_ref, out_ref)
 
 
 def after_kernel(in_ref, out_ref):
-    for half, owners in enumerate(OWNERS_AFTER):
-
-        @pl.when(in_half(Z_D, half))
-        def _():
-            acc = jnp.zeros((PIECE, 128), F32)
-            for b in reversed(range(SEQ)):
-                if b in owners:
-                    out_ref[owners.index(b)] = acc
-                acc = acc + in_ref[OUT_AFTER.index(b)]
+    running_sums(range(SEQ - 1, -1, -1), OUT_AFTER, BACK_AFTER, in_ref, out_ref)
 
 
 def attn_kernel(q_ref, k_ref, v_ref, gain_ref, go_ref, parts_ref, attn_ref, scaled_ref, sums_ref, state_ref):
-    for i, pair in enumerate(zip(*OWNERS_BEFORE)):
-        part = sum(parts_ref[BACK_BEFORE.index(owner)] for owner in pair)
-        state_ref[i * PIECE : (i + 1) * PIECE, :] = part.astype(BF16)
+    for p in range(PIECES):
+        state_ref[p * PIECE : (p + 1) * PIECE, :] = joined(parts_ref, p, BACK_BEFORE).astype(BF16)
     _, upper = masks()
     gain = jnp.broadcast_to(gain_ref[...].astype(F32)[None, :], (8, WIDTH)).T[:, 0:1]
     square = [jnp.zeros((8, TILE), F32) for _ in range(BLK // TILE)]
@@ -162,11 +189,7 @@
     for h in range(HEADS):
         g = (scaled_ref[head(h), :] * inv - attn_ref[head(h), :] * factor).astype(BF16)
         g_ref[head(h), :] = g
-        terms = nn(g, q_ref[:, head(h)])
-        for i in range(HD // PIECE):
-            part = terms[i * PIECE : (i + 1) * PIECE]
-            for owners in OWNERS_AFTER:
-                out_ref[OUT_AFTER.index(owners[h * (HD // PIECE) + i])] = part
+        spread(nn(g, q_ref[:, head(h)]), h, OUT_AFTER, out_ref)
 
 
 def inner_kernel(q_ref, k_ref, v_ref, g_ref, state_ref, gq_ref, gk_ref, gv_ref):
@@ -199,17 +222,20 @@
             gv_ref[tile(s), head(h)] = gv
 
 
-def last_kernel(k_ref, v_ref, gk_in_ref, gv_in_ref, state_ref, gk_hbm, gv_hbm, gk_ref, gv_ref, sems):
-    state = [state_ref[head(h), :].astype(BF16) for h in range(HEADS)]
+def last_kernel(k_ref, v_ref, gk_in_ref, gv_in_ref, parts_ref, gk_hbm, gv_hbm, gk_ref, gv_ref, sems):
+    parts = [joined(parts_ref, p, BACK_AFTER).astype(BF16) for p in range(PIECES)]
+    state = [jnp.concatenate(parts[h * PIECES // 2 : (h + 1) * PIECES // 2], axis=0) for h in range(HEADS)]
     copies = []
-    for t in range(BLK // TILE):
-        for h in range(HEADS):
-            gk = gk_in_ref[tile(t), head(h)] + nn(v_ref[tile(t), head(h)], state[h])
-            gk_ref[tile(t), head(h)] = gk.astype(BF16)
-            gv = gv_in_ref[tile(t), head(h)] + nt(k_ref[tile(t), head(h)], state[h])
-            gv_ref[tile(t), head(h)] = gv.astype(BF16)
+    for t in range(LAST_TILES):
+        rows = slice(t * BLK // LAST_TILES, (t + 1) * BLK // LAST_TILES)
         for i, (mine, out) in enumerate(((gk_ref, gk_hbm), (gv_ref, gv_hbm))):
-            copies.append(pltpu.make_async_copy(mine.at[tile(t)], out.at[tile(t)], sems.at[i, t]))
+            for h in range(HEADS):
+                if i == 0:
+                    grad = gk_in_ref[rows, head(h)] + nn(v_ref[rows, head(h)], state[h])
+                else:
+                    grad = gv_in_ref[rows, head(h)] + nt(k_ref[rows, head(h)], state[h])
+                mine[rows, head(h)] = grad.astype(BF16)
+            copies.append(pltpu.make_async_copy(mine.at[rows], out.at[rows], sems.at[i, t]))
             copies[-1].start()
     for copy in copies:
         copy.wait()
@@ -220,7 +246,7 @@
 
 
 def local(queries, keys, values, gain, grad_out):
-    state_shape = pltpu.VMEM((WIDTH, HD), F32)
+    piece_shape = pltpu.VMEM((HALF, PIECE, HD), F32)
     half = jax.ShapeDtypeStruct((BLK, WIDTH), BF16)
     full = jax.ShapeDtypeStruct((BLK, WIDTH), F32)
     half_turned = jax.ShapeDtypeStruct((WIDTH, BLK), BF16)
@@ -232,7 +258,7 @@
     )
     key_terms, gain = call(
         state_kernel,
-        (state_shape, pltpu.VMEM((WIDTH,), BF16)),
+        (piece_shape, pltpu.VMEM((WIDTH,), BF16)),
         small,
         2**19,
         in_specs=[pl.BlockSpec(memory_space=pltpu.HBM)] * 3,
@@ -242,9 +268,9 @@
             pltpu.SemaphoreType.DMA((3,)),
         ],
     )(keys_here, values_here, gain_here)
-    pieces = exchange(key_terms.reshape(HALF, PIECE, HD), "seq", OWNERS_BEFORE)
-    pieces = call(before_kernel, pltpu.VMEM((SEQ, PIECE, HD), F32), 2**16, 2**19)(pieces)
-    key_parts = exchange(pieces, "seq", [BACK_BEFORE])
+    pieces = exchange(key_terms, "seq", OUT_BEFORE)
+    pieces = call(before_kernel, piece_shape, 2**16, 2**19)(pieces)
+    key_parts = exchange(pieces, "seq", BACK_BEFORE)
     attn, scaled, sums, key_state = call(
         attn_kernel,
         (
@@ -258,13 +284,13 @@
     )(queries, keys, values, gain, grad_out, key_parts)
     sums = exchange(sums, "tp", [listed(TP, FIRST_TP)])
     grad_attn, query_terms = call(
-        grad_kernel, (half_turned, pltpu.VMEM((SEQ, PIECE, HD), F32)), small, 2**21
+        grad_kernel, (half_turned, piece_shape), small, 2**21
     )(
         queries, scaled, attn, sums
     )
-    pieces = exchange(query_terms, "seq", [OUT_AFTER])
-    pieces = call(after_kernel, pltpu.VMEM((HALF, PIECE, HD), F32), 2**16, 2**19)(pieces)
-    grad_state = exchange(pieces, "seq", OWNERS_AFTER).reshape(WIDTH, HD)
+    pieces = exchange(query_terms, "seq", OUT_AFTER)
+    pieces = call(after_kernel, piece_shape, 2**16, 2**19)(pieces)
+    grad_parts = exchange(pieces, "seq", BACK_AFTER)
     grad_q, inner_k, inner_v = call(inner_kernel, (half, full, full), 6 * square, 2**22)(
         queries, keys, values, grad_attn, key_state
     )
@@ -278,9 +304,9 @@
         scratch_shapes=[
             pltpu.VMEM((BLK, WIDTH), BF16),
             pltpu.VMEM((BLK, WIDTH), BF16),
-            pltpu.SemaphoreType.DMA((2, BLK // TILE)),
+            pltpu.SemaphoreType.DMA((2, LAST_TILES)),
         ],
-    )(keys, values, inner_k, inner_v, grad_state)
+    )(keys, values, inner_k, inner_v, grad_parts)
     return grad_q, grad_k, grad_v
 
 

time: 76.6 us -> 76.1 us (level)
  blocking collectives: 60 us -> 57.6 us
  waiting for transfers between devices: 3.59 us -> 5.05 us
    all_to_all x4, blocking collectives: 60 us -> 57.6 us  [exchange(): lax.all_to_all(pieces, axis, 0, 0, tiled=True, axis_index_groups=groups)]
    all_to_all x1, waiting for transfers between devices: 3.59 us -> 5.05 us  [exchange(): lax.all_to_all(pieces, axis, 0, 0, tiled=True, axis_index_groups=groups)]
where the time goes in v6:
time: 76.1 us; the launch traced here: 75.8 us
  blocking collectives  57.6 us (76%)
  Pallas kernels  6.62 us (9%)
  starting transfers between devices  5.78 us (8%)
  waiting for transfers between devices  5.05 us (7%)
    all_to_all x4, blocking collectives, exchange(): lax.all_to_all(pieces, axis, 0, 0, tiled=True, axis_index_groups=groups)  57.6 us
    all_to_all x1, starting transfers between devices, exchange(): lax.all_to_all(pieces, axis, 0, 0, tiled=True, axis_index_groups=groups)  5.78 us
    all_to_all x1, waiting for transfers between devices, exchange(): lax.all_to_all(pieces, axis, 0, 0, tiled=True, axis_index_groups=groups)  5.05 us
    pallas_call x1, Pallas kernels, local(): call(inner_kernel, (half, full, full), 6 * square, 2 ** 22)  2.37 us
  transfers between devices with their start and end apart: 1, of which 1 were waited for; matrix products, arithmetic and copies ran while one was open for 0% of the time, Pallas kernels for 3%

profile of v6, /device:TPU:6, one launch (start us, length us, event | category | flops | bytes accessed | tf_op | source)
XLA Modules:
  0.0 75.8 jit_solution(6833799698026251343)
XLA Ops:
  0.6 1.3 %shard_map.76 = (f32[16,32,128]{2,1,0:T(8,128)S(1)}, bf16[256]{0:T(256)(128)(2,1)S(1)}) custom-call(bf16[512,256]{1,0:T(8,128)(2,1)} %k_ref.5, bf16[512,256]{1,0:T(8,128)(2,1)} %v_ref.5, bf16[256]{0:T(256)(128)(2,1)} %gain_hbm.1), custom_call_target="tpu_custom_call" | custom-call | flops 33554432 | bytes 524288 | tf_op jit(solution)/shard_map/pallas_call | solution.py:259
  2.0 17.7 %all_to_all.25.in_ref = f32[16,32,128]{2,1,0:T(8,128)S(1)} all-to-all(f32[16,32,128]{2,1,0:T(8,128)S(1)} %get-tuple-element.17), channel_id=1, replica_groups={{96,112,128,144,160,176,192,208,224,240,0,16,32,48,64,80},{352,368,384,..., dimensions={0} | all-to-all | bytes 524288 | tf_op jit(solution)/shard_map/all_to_all | solution.py:245
  19.7 0.0 copy-start.2
  19.7 0.0 copy-start.3
  19.7 0.0 copy-start
  19.7 0.0 copy-start.1
  19.7 15.8 %all_to_all.26.parts_ref = f32[16,32,128]{2,1,0:T(8,128)S(1)} all-to-all(f32[16,32,128]{2,1,0:T(8,128)S(1)} %shard_map.77), channel_id=1, replica_groups={{288,304,320,336,352,368,128,144,160,176,192,208,224,240,256,272},{416,..., dimensions={0} | all-to-all | bytes 524288 | tf_op jit(solution)/shard_map/all_to_all | solution.py:245
  35.6 0.0 copy-done.2
  35.6 0.0 copy-done.3
  35.6 0.0 copy-done
  35.6 0.0 copy-done.1
  35.6 0.9 %shard_map.78 = (f32[256,512]{1,0:T(8,128)S(1)}, f32[256,512]{1,0:T(8,128)S(1)}, f32[16,8,128]{2,1,0:T(8,128)S(1)}, bf16[256,128]{1,0:T(8,128)(2,1)S(1)}) custom-call(bf16[512,256]{1,0:T(8,128)(2,1)S(1)} %copy-done.2, bf16[512,256]{1,0:T(8,128)(2,1)S(1)} %copy-done, bf16[512,256]{1,0:T(8,128)(2,1)S(1)} %copy-done.1, ...), custom_call_target="tpu_custom_call" | custom-call | flops 301989888 | bytes 2097152 | tf_op jit(solution)/shard_map/pallas_call | solution.py:274
  36.5 10.6 %all_to_all.27.sums_ref = f32[16,8,128]{2,1,0:T(8,128)S(1)} all-to-all(f32[16,8,128]{2,1,0:T(8,128)S(1)} %get-tuple-element.20), channel_id=1, replica_groups={{9,10,11,12,13,14,15,0,1,2,3,4,5,6,7,8},{25,26,27,28,29,30,31,16,17,18,..., dimensions={0} | all-to-all | bytes 131072 | tf_op jit(solution)/shard_map/all_to_all | solution.py:245
  47.1 0.3 shard_map.79
  47.4 13.5 %all_to_all.28.in_ref = f32[16,32,128]{2,1,0:T(8,128)S(1)} all-to-all(f32[16,32,128]{2,1,0:T(8,128)S(1)} %get-tuple-element.26), channel_id=1, replica_groups={{160,176,192,208,224,240,0,16,32,48,64,80,96,112,128,144},{416,432,448,..., dimensions={0} | all-to-all | bytes 524288 | tf_op jit(solution)/shard_map/all_to_all | solution.py:245
  60.8 0.7 shard_map.81
  61.6 5.8 %all-to-all-start.4 = ((f32[16,32,128]{2,1,0:T(8,128)}), f32[16,32,128]{2,1,0:T(8,128)S(1)}, u32[]{:S(2)}, u32[]{:S(2)}) async-start(f32[16,32,128]{2,1,0:T(8,128)} %shard_map.81), calls=%async_computation.4 | async-start | bytes 524288 | tf_op jit(solution)/shard_map/all_to_all | solution.py:245
  67.3 2.4 %shard_map.80 = (bf16[512,256]{1,0:T(8,128)(2,1)}, f32[512,256]{1,0:T(8,128)S(1)}, f32[512,256]{1,0:T(8,128)S(1)}) custom-call(bf16[512,256]{1,0:T(8,128)(2,1)S(1)} %copy-done.2, bf16[512,256]{1,0:T(8,128)(2,1)S(1)} %copy-done, bf16[512,256]{1,0:T(8,128)(2,1)S(1)} %copy-done.1, bf16[256,512]{1,0:T(8,128)(2,1)S(1)} %get-tuple-element.21.g_ref, ...), custom_call_target="tpu_custom_call" | custom-call | flops 805306368 | bytes 4194304 | tf_op jit(solution)/shard_map/pallas_call | solution.py:294
  69.7 5.0 %all-to-all-done.4.parts_ref = f32[16,32,128]{2,1,0:T(8,128)S(1)} async-done(((f32[16,32,128]{2,1,0:T(8,128)}), f32[16,32,128]{2,1,0:T(8,128)S(1)}, u32[]{:S(2)}, u32[]{:S(2)}) %all-to-all-start.4) | async-done | bytes 262176 | tf_op jit(solution)/shard_map/all_to_all | solution.py:245
  74.8 1.0 %shard_map.82 = (bf16[512,256]{1,0:T(8,128)(2,1)}, bf16[512,256]{1,0:T(8,128)(2,1)}) custom-call(bf16[512,256]{1,0:T(8,128)(2,1)S(1)} %copy-done, bf16[512,256]{1,0:T(8,128)(2,1)S(1)} %copy-done.1, f32[512,256]{1,0:T(8,128)S(1)} %get-tuple-element.24.gk_in_ref, f32[512,256]{1,0:T(8,128)S(1)} %get-tuple-element.25.gv_in_ref, ...), custom_call_target="tpu_custom_call" | custom-call | flops 67108864 | bytes 2097152 | tf_op jit(solution)/shard_map/pallas_call | solution.py:297
  (1 shorter events, 0.0 us)
Async XLA Ops:
  19.7 15.9 %copy-start.2 = (bf16[512,256]{1,0:T(8,128)(2,1)S(1)}, bf16[512,256]{1,0:T(8,128)(2,1)}, u32[]{:S(2)}) copy-start(bf16[512,256]{1,0:T(8,128)(2,1)} %q_ref.5) | copy-start | bytes 786436
  19.7 15.9 %copy-start.3 = (bf16[512,256]{1,0:T(8,128)(2,1)S(1)}, bf16[512,256]{1,0:T(8,128)(2,1)}, u32[]{:S(2)}) copy-start(bf16[512,256]{1,0:T(8,128)(2,1)} %go_ref.1) | copy-start | bytes 786436
  19.7 15.9 %copy-start = (bf16[512,256]{1,0:T(8,128)(2,1)S(1)}, bf16[512,256]{1,0:T(8,128)(2,1)}, u32[]{:S(2)}) copy-start(bf16[512,256]{1,0:T(8,128)(2,1)} %k_ref.5) | copy-start | bytes 786436
  19.7 15.9 %copy-start.1 = (bf16[512,256]{1,0:T(8,128)(2,1)S(1)}, bf16[512,256]{1,0:T(8,128)(2,1)}, u32[]{:S(2)}) copy-start(bf16[512,256]{1,0:T(8,128)(2,1)} %v_ref.5) | copy-start | bytes 786436
  61.6 13.2 %all-to-all-start.4 = ((f32[16,32,128]{2,1,0:T(8,128)}), f32[16,32,128]{2,1,0:T(8,128)S(1)}, u32[]{:S(2)}, u32[]{:S(2)}) async-start(f32[16,32,128]{2,1,0:T(8,128)} %shard_map.81), calls=%async_computation.4 | async-start | bytes 524288 | tf_op jit(solution)/shard_map/all_to_all | solution.py:245

commit v7 on v6

--- a/solution.py
+++ b/solution.py
@@ -13,20 +13,19 @@
 WIDTH = HEADS * HD
 SEQ = 32
 HALF = 16
+PIECE_BEFORE = 16
 PIECE = 32
 PIECES = WIDTH // PIECE
 TP = 16
 EPSILON = 1e-06
 LAST_TILES = 2
 Z_A = 0
-Z_B = 2
 Z_C = 0
 Z_D = 2
 FIRST_A = 6
-TURN_B = 8
 TURN_C = 0
 TURN_D = 0
-FIRST_B = 10
+FIRST_B = 22
 FIRST_TP = 9
 FIRST_C = 10
 FIRST_D = 6
@@ -83,7 +82,7 @@
 
 
 OUT_BEFORE = halves(Z_A, FIRST_A)
-BACK_BEFORE = halves(Z_B, FIRST_B, TURN_B)
+BACK_BEFORE = listed(SEQ, FIRST_B)
 OUT_AFTER = halves(Z_C, FIRST_C, TURN_C)
 BACK_AFTER = halves(Z_D, FIRST_D, TURN_D)
 
@@ -123,7 +122,9 @@
     turned = [v_ref[:, head(h)].T for h in range(HEADS)]
     copies[1].wait()
     for h in range(HEADS):
-        spread(nn(turned[h], k_ref[:, head(h)]), h, OUT_BEFORE, out_ref)
+        terms = nn(turned[h], k_ref[:, head(h)])
+        for i in range(HD // PIECE_BEFORE):
+            out_ref[h * (HD // PIECE_BEFORE) + i] = terms[i * PIECE_BEFORE : (i + 1) * PIECE_BEFORE]
     copies[2].wait()
 
 
@@ -142,7 +143,16 @@
 
 
 def before_kernel(in_ref, out_ref):
-    running_sums(range(SEQ), OUT_BEFORE, BACK_BEFORE, in_ref, out_ref)
+    place = lax.rem(lax.axis_index("seq") + (SEQ - 4 * Z_A), SEQ)
+    for half, owners in enumerate(OUT_BEFORE):
+
+        @pl.when(lax.div(place, HALF) == half)
+        def _():
+            acc = jnp.zeros((PIECE_BEFORE, 128), F32)
+            for b in range(SEQ):
+                out_ref[BACK_BEFORE.index(b)] = acc
+                if b in owners:
+                    acc = acc + in_ref[owners.index(b)]
 
 
 def after_kernel(in_ref, out_ref):
@@ -150,8 +160,9 @@
 
 
 def attn_kernel(q_ref, k_ref, v_ref, gain_ref, go_ref, parts_ref, attn_ref, scaled_ref, sums_ref, state_ref):
-    for p in range(PIECES):
-        state_ref[p * PIECE : (p + 1) * PIECE, :] = joined(parts_ref, p, BACK_BEFORE).astype(BF16)
+    for i, owners in enumerate(zip(*OUT_BEFORE)):
+        part = sum(parts_ref[BACK_BEFORE.index(owner)] for owner in owners)
+        state_ref[i * PIECE_BEFORE : (i + 1) * PIECE_BEFORE, :] = part.astype(BF16)
     _, upper = masks()
     gain = jnp.broadcast_to(gain_ref[...].astype(F32)[None, :], (8, WIDTH)).T[:, 0:1]
     square = [jnp.zeros((8, TILE), F32) for _ in range(BLK // TILE)]
@@ -258,7 +269,7 @@
     )
     key_terms, gain = call(
         state_kernel,
-        (piece_shape, pltpu.VMEM((WIDTH,), BF16)),
+        (pltpu.VMEM((HALF, PIECE_BEFORE, HD), F32), pltpu.VMEM((WIDTH,), BF16)),
         small,
         2**19,
         in_specs=[pl.BlockSpec(memory_space=pltpu.HBM)] * 3,
@@ -269,8 +280,9 @@
         ],
     )(keys_here, values_here, gain_here)
     pieces = exchange(key_terms, "seq", OUT_BEFORE)
-    pieces = call(before_kernel, piece_shape, 2**16, 2**19)(pieces)
-    key_parts = exchange(pieces, "seq", BACK_BEFORE)
+    sums_shape = pltpu.VMEM((SEQ, PIECE_BEFORE, HD), F32)
+    pieces = call(before_kernel, sums_shape, 2**16, 2**19)(pieces)
+    key_parts = exchange(pieces, "seq", [BACK_BEFORE])
     attn, scaled, sums, key_state = call(
         attn_kernel,
         (

time: 76.1 us -> 76.2 us (level)
  starting transfers between devices: 5.78 us -> 6.68 us
  blocking collectives: 57.6 us -> 56.8 us
    all_to_all x1, starting transfers between devices: 5.78 us -> 6.68 us  [exchange(): lax.all_to_all(pieces, axis, 0, 0, tiled=True, axis_index_groups=groups)]
    all_to_all x4, blocking collectives: 57.6 us -> 56.8 us  [exchange(): lax.all_to_all(pieces, axis, 0, 0, tiled=True, axis_index_groups=groups)]
where the time goes in v7:
time: 76.2 us; the launch traced here: 75.9 us
  blocking collectives  56.8 us (75%)
  starting transfers between devices  6.68 us (9%)
  Pallas kernels  6.62 us (9%)
  waiting for transfers between devices  5.04 us (7%)
    all_to_all x4, blocking collectives, exchange(): lax.all_to_all(pieces, axis, 0, 0, tiled=True, axis_index_groups=groups)  56.8 us
    all_to_all x1, starting transfers between devices, exchange(): lax.all_to_all(pieces, axis, 0, 0, tiled=True, axis_index_groups=groups)  6.68 us
    all_to_all x1, waiting for transfers between devices, exchange(): lax.all_to_all(pieces, axis, 0, 0, tiled=True, axis_index_groups=groups)  5.04 us
    pallas_call x1, Pallas kernels, local(): call(inner_kernel, (half, full, full), 6 * square, 2 ** 22)  2.38 us
  transfers between devices with their start and end apart: 1, of which 1 were waited for; matrix products, arithmetic and copies ran while one was open for 0% of the time, Pallas kernels for 3%

profile of v7, /device:TPU:6, one launch (start us, length us, event | category | flops | bytes accessed | tf_op | source)
XLA Modules:
  0.0 75.9 jit_solution(171188467402683728)
XLA Ops:
  0.6 1.3 %shard_map.76 = (f32[16,16,128]{2,1,0:T(8,128)S(1)}, bf16[256]{0:T(256)(128)(2,1)S(1)}) custom-call(bf16[512,256]{1,0:T(8,128)(2,1)} %k_ref.5, bf16[512,256]{1,0:T(8,128)(2,1)} %v_ref.5, bf16[256]{0:T(256)(128)(2,1)} %gain_hbm.1), custom_call_target="tpu_custom_call" | custom-call | flops 33554432 | bytes 524288 | tf_op jit(solution)/shard_map/pallas_call | solution.py:270
  2.0 0.0 copy-start.3
  2.0 15.7 %all_to_all.25.in_ref = f32[16,16,128]{2,1,0:T(8,128)S(1)} all-to-all(f32[16,16,128]{2,1,0:T(8,128)S(1)} %get-tuple-element.17), channel_id=1, replica_groups={{96,112,128,144,160,176,192,208,224,240,0,16,32,48,64,80},{352,368,384,..., dimensions={0} | all-to-all | bytes 262144 | tf_op jit(solution)/shard_map/all_to_all | solution.py:256
  17.7 0.0 copy-start.2
  17.7 0.0 copy-start
  17.8 0.0 copy-start.1
  17.8 17.0 %all_to_all.26.parts_ref = f32[32,16,128]{2,1,0:T(8,128)S(1)} all-to-all(f32[32,16,128]{2,1,0:T(8,128)S(1)} %shard_map.77), channel_id=1, replica_groups={{352,368,384,400,416,432,448,464,480,496,0,16,32,48,64,80,96,112,128,14..., dimensions={0} | all-to-all | bytes 524288 | tf_op jit(solution)/shard_map/all_to_all | solution.py:256
  34.8 0.0 copy-done.3
  34.8 0.0 copy-done.2
  34.8 0.0 copy-done
  34.8 0.0 copy-done.1
  34.8 0.9 %shard_map.78 = (f32[256,512]{1,0:T(8,128)S(1)}, f32[256,512]{1,0:T(8,128)S(1)}, f32[16,8,128]{2,1,0:T(8,128)S(1)}, bf16[256,128]{1,0:T(8,128)(2,1)S(1)}) custom-call(bf16[512,256]{1,0:T(8,128)(2,1)S(1)} %copy-done.2, bf16[512,256]{1,0:T(8,128)(2,1)S(1)} %copy-done, bf16[512,256]{1,0:T(8,128)(2,1)S(1)} %copy-done.1, ...), custom_call_target="tpu_custom_call" | custom-call | flops 301989888 | bytes 2097152 | tf_op jit(solution)/shard_map/pallas_call | solution.py:286
  35.7 10.6 %all_to_all.27.sums_ref = f32[16,8,128]{2,1,0:T(8,128)S(1)} all-to-all(f32[16,8,128]{2,1,0:T(8,128)S(1)} %get-tuple-element.20), channel_id=1, replica_groups={{9,10,11,12,13,14,15,0,1,2,3,4,5,6,7,8},{25,26,27,28,29,30,31,16,17,18,..., dimensions={0} | all-to-all | bytes 131072 | tf_op jit(solution)/shard_map/all_to_all | solution.py:256
  46.3 0.3 shard_map.79
  46.6 13.5 %all_to_all.28.in_ref = f32[16,32,128]{2,1,0:T(8,128)S(1)} all-to-all(f32[16,32,128]{2,1,0:T(8,128)S(1)} %get-tuple-element.26), channel_id=1, replica_groups={{160,176,192,208,224,240,0,16,32,48,64,80,96,112,128,144},{416,432,448,..., dimensions={0} | all-to-all | bytes 524288 | tf_op jit(solution)/shard_map/all_to_all | solution.py:256
  60.0 0.7 shard_map.81
  60.7 6.7 %all-to-all-start.4 = ((f32[16,32,128]{2,1,0:T(8,128)}), f32[16,32,128]{2,1,0:T(8,128)S(1)}, u32[]{:S(2)}, u32[]{:S(2)}) async-start(f32[16,32,128]{2,1,0:T(8,128)} %shard_map.81), calls=%async_computation.4 | async-start | bytes 524288 | tf_op jit(solution)/shard_map/all_to_all | solution.py:256
  67.4 2.4 %shard_map.80 = (bf16[512,256]{1,0:T(8,128)(2,1)}, f32[512,256]{1,0:T(8,128)S(1)}, f32[512,256]{1,0:T(8,128)S(1)}) custom-call(bf16[512,256]{1,0:T(8,128)(2,1)S(1)} %copy-done.2, bf16[512,256]{1,0:T(8,128)(2,1)S(1)} %copy-done, bf16[512,256]{1,0:T(8,128)(2,1)S(1)} %copy-done.1, bf16[256,512]{1,0:T(8,128)(2,1)S(1)} %get-tuple-element.21.g_ref, ...), custom_call_target="tpu_custom_call" | custom-call | flops 805306368 | bytes 4194304 | tf_op jit(solution)/shard_map/pallas_call | solution.py:306
  69.8 5.0 %all-to-all-done.4.parts_ref = f32[16,32,128]{2,1,0:T(8,128)S(1)} async-done(((f32[16,32,128]{2,1,0:T(8,128)}), f32[16,32,128]{2,1,0:T(8,128)S(1)}, u32[]{:S(2)}, u32[]{:S(2)}) %all-to-all-start.4) | async-done | bytes 262176 | tf_op jit(solution)/shard_map/all_to_all | solution.py:256
  74.8 1.0 %shard_map.82 = (bf16[512,256]{1,0:T(8,128)(2,1)}, bf16[512,256]{1,0:T(8,128)(2,1)}) custom-call(bf16[512,256]{1,0:T(8,128)(2,1)S(1)} %copy-done, bf16[512,256]{1,0:T(8,128)(2,1)S(1)} %copy-done.1, f32[512,256]{1,0:T(8,128)S(1)} %get-tuple-element.24.gk_in_ref, f32[512,256]{1,0:T(8,128)S(1)} %get-tuple-element.25.gv_in_ref, ...), custom_call_target="tpu_custom_call" | custom-call | flops 67108864 | bytes 2097152 | tf_op jit(solution)/shard_map/pallas_call | solution.py:309
  (1 shorter events, 0.0 us)
Async XLA Ops:
  2.0 32.8 %copy-start.3 = (bf16[512,256]{1,0:T(8,128)(2,1)S(1)}, bf16[512,256]{1,0:T(8,128)(2,1)}, u32[]{:S(2)}) copy-start(bf16[512,256]{1,0:T(8,128)(2,1)} %go_ref.1) | copy-start | bytes 786436
  17.7 17.1 %copy-start.2 = (bf16[512,256]{1,0:T(8,128)(2,1)S(1)}, bf16[512,256]{1,0:T(8,128)(2,1)}, u32[]{:S(2)}) copy-start(bf16[512,256]{1,0:T(8,128)(2,1)} %q_ref.5) | copy-start | bytes 786436
  17.7 17.0 %copy-start = (bf16[512,256]{1,0:T(8,128)(2,1)S(1)}, bf16[512,256]{1,0:T(8,128)(2,1)}, u32[]{:S(2)}) copy-start(bf16[512,256]{1,0:T(8,128)(2,1)} %k_ref.5) | copy-start | bytes 786436
  17.8 17.0 %copy-start.1 = (bf16[512,256]{1,0:T(8,128)(2,1)S(1)}, bf16[512,256]{1,0:T(8,128)(2,1)}, u32[]{:S(2)}) copy-start(bf16[512,256]{1,0:T(8,128)(2,1)} %v_ref.5) | copy-start | bytes 786436
  60.7 14.1 %all-to-all-start.4 = ((f32[16,32,128]{2,1,0:T(8,128)}), f32[16,32,128]{2,1,0:T(8,128)S(1)}, u32[]{:S(2)}, u32[]{:S(2)}) async-start(f32[16,32,128]{2,1,0:T(8,128)} %shard_map.81), calls=%async_computation.4 | async-start | bytes 524288 | tf_op jit(solution)/shard_map/all_to_all | solution.py:256
